TPU v7x, 512 devices: a whole 4x4x16 slice. The times are simulated.
512 devices in a mesh: gx: 8 (over z_lo, core), vert: 64 (over y, x, z_hi).
Axes of the slice: x: 4, y: 4, z: 16 (z_hi: 4, z_lo: 4; z = z_hi * 4 + z_lo), core: 2. Of those that a mesh axis runs over, the one named last changes fastest.
Arguments:
- density_start: float32 [64, 16, 16, 32, 128], P('vert', None, None, 'gx'), may hold values from 0.05 to 18, as said below
- value_guess: float32 [64, 16, 16, 32, 128], P('vert', None, None, 'gx'), may hold values from -6 to 6
- value_end: float32 [64, 16, 16, 32, 128], P('vert', None, None, 'gx'), may hold values from -6 to 6
- walls: int32 [32, 128], P('gx'), may hold values from 0 to 1, as said below
Outputs:
- density_end: float32 [64, 16, 16, 32, 128], P('vert', None, None, 'gx')
- value_start: float32 [64, 16, 16, 32, 128], P('vert', None, None, 'gx')
Inputs may be any that keep to these rules, and one draw needn't show every extreme that they name: `walls`: each row of fixed x holds exactly 32 wall cells. `density_start`: A positive density.
All inputs are finite; a program needn't handle non-finite values.
Results may differ from a plain program's by a relative error of at most 0.00002.
Values sent between devices are 32-bit elements; how exact they have to be, the bound alone decides.
A program may use at most 64 MiB of HBM per device.

v0:
```python
import jax
import jax.numpy as jnp
from jax import lax
from jax.sharding import PartitionSpec as P

VX = 128
VY = 128
KY = 8


advect_rate = 0.3
diffusion = 0.05
drift_limit = 0.1
control_gain = 1.0
alignment = 1.0
hamilton_rate = 0.05
time_step = 0.2
density_cost = 2.0
velocity_cost = 1.0


def from_behind(x, axis, by):
    size = lax.axis_size(axis)
    pairs = [(i, i + by) for i in range(size) if 0 <= i + by < size]
    return lax.ppermute(x, axis, pairs)


def with_halo(cells, sides, width):
    for axis, dim in sides:
        count = lax.axis_size(axis)
        head = lax.slice_in_dim(cells, 0, width, axis=dim)
        tail = lax.slice_in_dim(cells, cells.shape[dim] - width, cells.shape[dim], axis=dim)
        cells = jnp.concatenate(
            [
                lax.ppermute(tail, axis, [(i, (i + 1) % count) for i in range(count)]),
                cells,
                lax.ppermute(head, axis, [((i + 1) % count, i) for i in range(count)]),
            ],
            axis=dim,
        )
    return cells


def partner_2(block, axis, distance):
    count = lax.axis_size(axis)
    route = []
    for low in range(count):
        high = low | 1 << distance
        if high != low and high < count:
            route += [(low, high), (high, low)]
    return lax.ppermute(block, axis, route)


def bit_order():
    return list(range(KY.bit_length() - 1))


def neighbours(up_x, down_x, up_y, down_y, vy_block):
    from_below_x = from_behind(up_x[:, -1:], "vert", KY)
    from_above_x = from_behind(down_x[:, :1], "vert", -KY)
    from_below_y = from_behind(up_y[:, :, -1:], "vert", 1)
    from_above_y = from_behind(down_y[:, :, :1], "vert", -1)
    from_below_y = jnp.where(vy_block == 0, 0.0, from_below_y)
    from_above_y = jnp.where(vy_block == KY - 1, 0.0, from_above_y)
    lower_x = jnp.concatenate([from_below_x, up_x[:, :-1]], axis=1)
    upper_x = jnp.concatenate([down_x[:, 1:], from_above_x], axis=1)
    lower_y = jnp.concatenate([from_below_y, up_y[:, :, :-1]], axis=2)
    upper_y = jnp.concatenate([down_y[:, :, 1:], from_above_y], axis=2)
    return (lower_x, upper_x, lower_y, upper_y)


def x_neighbours(field):
    extended = with_halo(field, (("gx", 3),), 1)
    return (extended[:, :, :, :-2], extended[:, :, :, 2:])


def moment_stats(field, vx_hat, vy_hat):
    total = jnp.sum(field, axis=(0, 1, 2))
    mom_x = jnp.sum(vx_hat * field, axis=(0, 1, 2))
    mom_y = jnp.sum(vy_hat * field, axis=(0, 1, 2))
    total, mom_x, mom_y = lax.psum((total, mom_x, mom_y), "vert")
    return (total, mom_x / total, mom_y / total)


def reflect(field, wall_cells):
    partner = field[:, :, ::-1]
    for bit_index in bit_order():
        partner = partner_2(partner, "vert", bit_index)
    return jnp.where(wall_cells, 0.5 * (field + partner), field)


def blocks_path(density_start, value_guess, value_end, walls):
    position = lax.axis_index("vert")
    vx_block = position // KY
    vy_block = position % KY
    block_x = density_start.shape[1]
    block_y = density_start.shape[2]
    vx_index = (vx_block * block_x + jnp.arange(block_x, dtype=jnp.int32)).astype(jnp.float32)
    vy_index = (vy_block * block_y + jnp.arange(block_y, dtype=jnp.int32)).astype(jnp.float32)
    vx_hat = ((vx_index - (VX - 1) / 2.0) / (VX / 2.0)).reshape(1, block_x, 1, 1, 1)
    vy_hat = ((vy_index - (VY - 1) / 2.0) / (VY / 2.0)).reshape(1, 1, block_y, 1, 1)
    wall_cells = (walls == 1)[None, None, None]
    speed_x = advect_rate * vx_hat
    speed_y = advect_rate * vy_hat
    lower_gx, upper_gx, lower_gy, upper_gy = neighbours(
        value_guess, value_guess, value_guess, value_guess, vy_block
    )
    grad_x = 0.5 * (upper_gx - lower_gx)
    grad_y = 0.5 * (upper_gy - lower_gy)

    def forward_step(field, stats):
        total, mean_x, mean_y = stats
        drift_x = drift_limit * jnp.tanh(-control_gain * grad_x + alignment * (mean_x - vx_hat))
        drift_y = drift_limit * jnp.tanh(-control_gain * grad_y + alignment * (mean_y - vy_hat))
        push_x = jnp.maximum(drift_x, 0.0) * field
        pull_x = jnp.minimum(drift_x, 0.0) * field
        push_y = jnp.maximum(drift_y, 0.0) * field
        pull_y = jnp.minimum(drift_y, 0.0) * field
        spread = diffusion * field
        lower_x, upper_x, lower_y, upper_y = neighbours(
            spread + push_x, spread - pull_x, spread + push_y, spread - pull_y, vy_block
        )
        velocity_part = (
            lower_x + upper_x + lower_y + upper_y - 4.0 * spread - push_x + pull_x - push_y + pull_y
        )
        before_x, after_x = x_neighbours(field)
        transport = (
            jnp.maximum(speed_x, 0.0) * (field - before_x)
            + jnp.minimum(speed_x, 0.0) * (after_x - field)
            + jnp.maximum(speed_y, 0.0) * (field - jnp.roll(field, 1, axis=4))
            + jnp.minimum(speed_y, 0.0) * (jnp.roll(field, -1, axis=4) - field)
        )
        return reflect(field + velocity_part - transport, wall_cells)

    def backward_step(value, stats):
        total, mean_x, mean_y = stats
        below_x, above_x, below_y, above_y = neighbours(value, value, value, value, vy_block)
        grad_vx = 0.5 * (above_x - below_x)
        grad_vy = 0.5 * (above_y - below_y)
        laplace = above_x + below_x + above_y + below_y - 4.0 * value
        before_x, after_x = x_neighbours(value)
        transport = (
            jnp.maximum(speed_x, 0.0) * (after_x - value)
            + jnp.minimum(speed_x, 0.0) * (value - before_x)
            + jnp.maximum(speed_y, 0.0) * (jnp.roll(value, -1, axis=4) - value)
            + jnp.minimum(speed_y, 0.0) * (value - jnp.roll(value, 1, axis=4))
        )
        density = total / (VX * VY)
        offset_x = vx_hat - mean_x
        offset_y = vy_hat - mean_y
        running = density_cost * density + 0.5 * velocity_cost * (
            offset_x * offset_x + offset_y * offset_y
        )
        updated = (
            value
            + transport
            - hamilton_rate * (grad_vx * grad_vx + grad_vy * grad_vy)
            + diffusion * laplace
            + time_step * running
        )
        return reflect(updated, wall_cells)

    stats_start = moment_stats(density_start, vx_hat, vy_hat)
    field_one = forward_step(density_start, stats_start)
    stats_one = moment_stats(field_one, vx_hat, vy_hat)
    field_two = forward_step(field_one, stats_one)
    stats_two = moment_stats(field_two, vx_hat, vy_hat)
    value_one = backward_step(value_end, stats_two)
    value_zero = backward_step(value_one, stats_one)
    return (field_two, value_zero)


def per_device(density_start, value_guess, value_end, walls):
    return blocks_path(density_start, value_guess, value_end, walls)


def solution(mesh):
    return jax.shard_map(
        per_device,
        mesh=mesh,
        in_specs=(
            P("vert", None, None, "gx", None),
            P("vert", None, None, "gx", None),
            P("vert", None, None, "gx", None),
            P("gx", None),
        ),
        out_specs=(P("vert", None, None, "gx", None), P("vert", None, None, "gx", None)),
        check_vma=False,
    )
```

profile of v0, /device:TPU:1, one launch (start us, length us, event | category | flops | bytes accessed | tf_op | source)
XLA Modules:
  0.0 1215.1 jit_solution(9652615527141164823)
XLA Ops:
  1.5 9.6 collective-permute-start.5
  11.1 1.3 collective-permute-start.4
  12.4 1.4 fusion.100
  13.8 1.3 collective-permute-start
  15.1 9.5 collective-permute-start.1
  24.6 2.2 fusion.101
  26.9 3.8 collective-permute-start.8
  33.9 1.3 fusion.96
  35.6 197.6 %all-reduce.2 = (f32[4,128]{1,0:T(4,128)S(1)}, f32[4,128]{1,0:T(4,128)S(1)}, f32[4,128]{1,0:T(4,128)S(1)}) all-reduce(f32[4,128]{1,0:T(4,128)S(1)} %get-tuple-element.10, f32[4,128]{1,0:T(4,128)S(1)} %get-tuple-element.9, f32[4,128]{1,0:T(4,128)S(1)} %get-tuple-element.8), channel_id=1, replica_groups=mesh['gx'=8,'vert'=64] {'vert'}, use_global_device_ids=true, to_apply=%region_1.2 | all-reduce | flops 1536 | bytes 12288 | tf_op jit(solution)/shard_map/psum | solution.py:81
  234.0 29.1 %collective-permute-start.9 = (f32[1,16,16,1,128]{4,3,2,1,0:T(1,128)S(1)}, f32[1,16,16,1,128]{4,3,2,1,0:T(1,128)S(1)}, u32[]{:S(2)}, u32[]{:S(2)}) collective-permute-start(f32[1,16,16,1,128]{4,3,2,1,0:T(1,128)S(1)} %get-tuple-element.80), channel_id=1, source_target_pairs={{64,0},{128,64},{192,128},{256,192},{320,256},{384,320},{448,384},... | collective-permute-start | bytes 393224 | tf_op jit(solution)/shard_map/ppermute | solution.py:37
  265.0 1.3 collective-permute-start.6
  267.6 1.4 collective-permute-start.2
  269.1 1.3 collective-permute-start.3
  270.4 1.3 collective-permute-start.7
  271.7 7.2 collective-permute-done.7
  279.7 2.5 fusion.35
  282.3 5.3 collective-permute-start.10
  287.6 59.0 %collective-permute-done.10 = f32[1,16,16,4,128]{4,3,2,1,0:T(4,128)S(1)} collective-permute-done((f32[1,16,16,4,128]{4,3,2,1,0:T(4,128)S(1)}, f32[1,16,16,4,128]{4,3,2,1,0:T(4,128)S(1)}, u32[]{:S(2)}, u32[]{:S(2)}) %collective-permute-start.10) | collective-permute-done | bytes 524320 | tf_op jit(solution)/shard_map/ppermute | solution.py:51
  346.6 6.2 collective-permute-start.11
  352.8 24.5 %collective-permute-done.11 = f32[1,16,16,4,128]{4,3,2,1,0:T(4,128)S(1)} collective-permute-done((f32[1,16,16,4,128]{4,3,2,1,0:T(4,128)S(1)}, f32[1,16,16,4,128]{4,3,2,1,0:T(4,128)S(1)}, u32[]{:S(2)}, u32[]{:S(2)}) %collective-permute-start.11) | collective-permute-done | bytes 524320 | tf_op jit(solution)/shard_map/ppermute | solution.py:51
  377.3 1.9 collective-permute-start.12
  379.9 19.0 %collective-permute-start.27 = (f32[1,16,1,4,128]{4,3,2,1,0:T(4,128)}, f32[1,16,1,4,128]{4,3,2,1,0:T(4,128)}, u32[]{:S(2)}, u32[]{:S(2)}) collective-permute-start(f32[1,16,1,4,128]{4,3,2,1,0:T(4,128)} %get-tuple-element.51), channel_id=1, source_target_pairs={{0,1},{1,2},{2,3},{3,4},{4,5},{5,6},{6,7},{7,8},{8,9},{9,10},{10,1... | collective-permute-start | bytes 98312 | tf_op jit(solution)/shard_map/ppermute | solution.py:25
  402.7 198.8 %all-reduce.1 = (f32[4,128]{1,0:T(4,128)S(1)}, f32[4,128]{1,0:T(4,128)S(1)}, f32[4,128]{1,0:T(4,128)S(1)}) all-reduce(f32[4,128]{1,0:T(4,128)S(1)} %get-tuple-element.7, f32[4,128]{1,0:T(4,128)S(1)} %get-tuple-element.6, f32[4,128]{1,0:T(4,128)S(1)} %get-tuple-element.5), channel_id=1, replica_groups=mesh['gx'=8,'vert'=64] {'vert'}, use_global_device_ids=true, to_apply=%region_7.8 | all-reduce | flops 1536 | bytes 12288 | tf_op jit(solution)/shard_map/psum | solution.py:81
  603.1 1.3 collective-permute-start.16
  604.9 8.0 collective-permute-start.15
  612.9 1.3 collective-permute-start.13
  614.2 1.3 collective-permute-start.14
  615.5 2.0 collective-permute-start.17
  617.5 31.2 %collective-permute-start.18 = (f32[1,16,16,1,128]{4,3,2,1,0:T(1,128)S(1)}, f32[1,16,16,1,128]{4,3,2,1,0:T(1,128)S(1)}, u32[]{:S(2)}, u32[]{:S(2)}) collective-permute-start(f32[1,16,16,1,128]{4,3,2,1,0:T(1,128)S(1)} %get-tuple-element.65), channel_id=1, source_target_pairs={{64,0},{128,64},{192,128},{256,192},{320,256},{384,320},{448,384},... | collective-permute-start | bytes 393224 | tf_op jit(solution)/shard_map/ppermute | solution.py:37
  648.8 1.3 collective-permute-start.26
  650.1 5.4 collective-permute-start.22
  655.5 1.9 collective-permute-start.23
  658.2 2.5 fusion.27
  660.7 8.2 collective-permute-start.19
  670.4 43.3 %collective-permute-done.19 = f32[1,16,16,4,128]{4,3,2,1,0:T(4,128)S(1)} collective-permute-done((f32[1,16,16,4,128]{4,3,2,1,0:T(4,128)S(1)}, f32[1,16,16,4,128]{4,3,2,1,0:T(4,128)S(1)}, u32[]{:S(2)}, u32[]{:S(2)}) %collective-permute-start.19) | collective-permute-done | bytes 524320 | tf_op jit(solution)/shard_map/ppermute | solution.py:51
  713.8 15.9 %collective-permute-start.20 = (f32[1,16,16,4,128]{4,3,2,1,0:T(4,128)S(1)}, f32[1,16,16,4,128]{4,3,2,1,0:T(4,128)S(1)}, u32[]{:S(2)}, u32[]{:S(2)}) collective-permute-start(f32[1,16,16,4,128]{4,3,2,1,0:T(4,128)S(1)} %collective-permute-done.19), channel_id=1, source_target_pairs={{0,2},{2,0},{1,3},{3,1},{4,6},{6,4},{5,7},{7,5},{8,10},{10,8},{9,1... | collective-permute-start | bytes 1572872 | tf_op jit(solution)/shard_map/ppermute | solution.py:51
  732.0 18.1 %collective-permute-done.20 = f32[1,16,16,4,128]{4,3,2,1,0:T(4,128)S(1)} collective-permute-done((f32[1,16,16,4,128]{4,3,2,1,0:T(4,128)S(1)}, f32[1,16,16,4,128]{4,3,2,1,0:T(4,128)S(1)}, u32[]{:S(2)}, u32[]{:S(2)}) %collective-permute-start.20) | collective-permute-done | bytes 524320 | tf_op jit(solution)/shard_map/ppermute | solution.py:51
  750.1 12.1 collective-permute-start.21
  762.8 1.3 collective-permute-start.24
  764.1 6.1 collective-permute-start.25
  771.0 1.9 collective-permute-done.21
  772.8 1.9 multiply_reduce_fusion.1
  775.4 203.1 %all-reduce = (f32[4,128]{1,0:T(4,128)S(1)}, f32[4,128]{1,0:T(4,128)S(1)}, f32[4,128]{1,0:T(4,128)S(1)}) all-reduce(f32[4,128]{1,0:T(4,128)S(1)} %copy-done.23, f32[4,128]{1,0:T(4,128)} %get-tuple-element.4, f32[4,128]{1,0:T(4,128)S(1)} %copy-done.22), channel_id=1, replica_groups=mesh['gx'=8,'vert'=64] {'vert'}, use_global_device_ids=true, to_apply=%region_17.18 | all-reduce | flops 1536 | bytes 12288 | tf_op jit(solution)/shard_map/psum | solution.py:81
  979.4 3.7 fusion.19
  983.2 1.9 collective-permute-start.28
  985.1 15.5 %collective-permute-done.28 = f32[1,16,16,4,128]{4,3,2,1,0:T(4,128)S(1)} collective-permute-done((f32[1,16,16,4,128]{4,3,2,1,0:T(4,128)S(1)}, f32[1,16,16,4,128]{4,3,2,1,0:T(4,128)S(1)}, u32[]{:S(2)}, u32[]{:S(2)}) %collective-permute-start.28) | collective-permute-done | bytes 524320 | tf_op jit(solution)/shard_map/ppermute | solution.py:51
  1000.5 8.7 collective-permute-start.29
  1009.2 15.3 %collective-permute-done.29 = f32[1,16,16,4,128]{4,3,2,1,0:T(4,128)S(1)} collective-permute-done((f32[1,16,16,4,128]{4,3,2,1,0:T(4,128)S(1)}, f32[1,16,16,4,128]{4,3,2,1,0:T(4,128)S(1)}, u32[]{:S(2)}, u32[]{:S(2)}) %collective-permute-start.29) | collective-permute-done | bytes 524320 | tf_op jit(solution)/shard_map/ppermute | solution.py:51
  1024.5 12.5 %collective-permute-start.30 = (f32[1,16,16,4,128]{4,3,2,1,0:T(4,128)S(1)}, f32[1,16,16,4,128]{4,3,2,1,0:T(4,128)S(1)}, u32[]{:S(2)}, u32[]{:S(2)}) collective-permute-start(f32[1,16,16,4,128]{4,3,2,1,0:T(4,128)S(1)} %collective-permute-done.29), channel_id=1, source_target_pairs={{0,4},{4,0},{1,5},{5,1},{2,6},{6,2},{3,7},{7,3},{8,12},{12,8},{9,1... | collective-permute-start | bytes 1572872 | tf_op jit(solution)/shard_map/ppermute | solution.py:51
  1037.0 6.8 collective-permute-done.30
  1045.4 1.3 collective-permute-start.36
  1046.7 50.0 %collective-permute-start.31 = (f32[1,16,16,1,128]{4,3,2,1,0:T(1,128)S(1)}, f32[1,16,16,1,128]{4,3,2,1,0:T(1,128)S(1)}, u32[]{:S(2)}, u32[]{:S(2)}) collective-permute-start(f32[1,16,16,1,128]{4,3,2,1,0:T(1,128)S(1)} %get-tuple-element.42), channel_id=1, source_target_pairs={{64,0},{128,64},{192,128},{256,192},{320,256},{384,320},{448,384},... | collective-permute-start | bytes 393224 | tf_op jit(solution)/shard_map/ppermute | solution.py:37
  1096.7 1.9 collective-permute-start.32
  1098.6 1.3 collective-permute-start.35
  1099.9 1.3 collective-permute-start.33
  1101.2 5.5 collective-permute-start.34
  1106.7 1.6 collective-permute-done.35
  1109.1 2.4 fusion.8
  1111.6 23.7 %collective-permute-start.37 = (f32[1,16,16,4,128]{4,3,2,1,0:T(4,128)S(1)}, f32[1,16,16,4,128]{4,3,2,1,0:T(4,128)S(1)}, u32[]{:S(2)}, u32[]{:S(2)}) collective-permute-start(f32[1,16,16,4,128]{4,3,2,1,0:T(4,128)S(1)} %rev.15), channel_id=1, source_target_pairs={{0,1},{1,0},{2,3},{3,2},{4,5},{5,4},{6,7},{7,6},{8,9},{9,8},{10,11... | collective-permute-start | bytes 1572872 | tf_op jit(solution)/shard_map/ppermute | solution.py:51
  1135.3 21.8 %collective-permute-done.37 = f32[1,16,16,4,128]{4,3,2,1,0:T(4,128)S(1)} collective-permute-done((f32[1,16,16,4,128]{4,3,2,1,0:T(4,128)S(1)}, f32[1,16,16,4,128]{4,3,2,1,0:T(4,128)S(1)}, u32[]{:S(2)}, u32[]{:S(2)}) %collective-permute-start.37) | collective-permute-done | bytes 524320 | tf_op jit(solution)/shard_map/ppermute | solution.py:51
  1157.1 8.8 collective-permute-start.38
  1166.0 25.3 %collective-permute-done.38 = f32[1,16,16,4,128]{4,3,2,1,0:T(4,128)S(1)} collective-permute-done((f32[1,16,16,4,128]{4,3,2,1,0:T(4,128)S(1)}, f32[1,16,16,4,128]{4,3,2,1,0:T(4,128)S(1)}, u32[]{:S(2)}, u32[]{:S(2)}) %collective-permute-start.38) | collective-permute-done | bytes 524320 | tf_op jit(solution)/shard_map/ppermute | solution.py:51
  1191.3 11.0 collective-permute-start.39
  1202.3 11.8 collective-permute-done.39
  (153 shorter events, 26.3 us)
Async XLA Ops:
  0.6 30.0 %copy-start.2 = (f32[1,16,16,4,128]{4,3,2,1,0:T(4,128)S(1)}, f32[1,16,16,4,128]{4,3,2,1,0:T(4,128)}, u32[]{:S(2)}) copy-start(f32[1,16,16,4,128]{4,3,2,1,0:T(4,128)} %param.5) | copy-start | bytes 1572868
  1.5 232.5 %collective-permute-start.5 = (f32[1,16,1,4,128]{4,3,2,1,0:T(4,128)S(1)}, f32[1,16,1,4,128]{4,3,2,1,0:T(4,128)S(1)}, u32[]{:S(2)}, u32[]{:S(2)}) collective-permute-start(f32[1,16,1,4,128]{4,3,2,1,0:T(4,128)S(1)} %get-tuple-element.74), channel_id=1, source_target_pairs={{0,1},{1,2},{2,3},{3,4},{4,5},{5,6},{6,7},{7,8},{8,9},{9,10},{10,1... | collective-permute-start | bytes 98312 | tf_op jit(solution)/shard_map/ppermute | solution.py:25
  11.1 252.0 %collective-permute-start.4 = (f32[1,16,1,4,128]{4,3,2,1,0:T(4,128)S(1)}, f32[1,16,1,4,128]{4,3,2,1,0:T(4,128)S(1)}, u32[]{:S(2)}, u32[]{:S(2)}) collective-permute-start(f32[1,16,1,4,128]{4,3,2,1,0:T(4,128)S(1)} %get-tuple-element.73), channel_id=1, source_target_pairs={{1,0},{2,1},{3,2},{4,3},{5,4},{6,5},{7,6},{8,7},{9,8},{10,9},{11,1... | collective-permute-start | bytes 98312 | tf_op jit(solution)/shard_map/ppermute | solution.py:25
  13.8 249.8 %collective-permute-start = (f32[1,1,16,4,128]{4,3,2,1,0:T(4,128)}, f32[1,1,16,4,128]{4,3,2,1,0:T(4,128)S(1)}, u32[]{:S(2)}, u32[]{:S(2)}) collective-permute-start(f32[1,1,16,4,128]{4,3,2,1,0:T(4,128)} %get-tuple-element.77), channel_id=1, source_target_pairs={{8,0},{9,1},{10,2},{11,3},{12,4},{13,5},{14,6},{15,7},{16,8},{17,9... | collective-permute-start | bytes 98312 | tf_op jit(solution)/shard_map/ppermute | solution.py:25
  15.1 248.5 %collective-permute-start.1 = (f32[1,1,16,4,128]{4,3,2,1,0:T(4,128)}, f32[1,1,16,4,128]{4,3,2,1,0:T(4,128)S(1)}, u32[]{:S(2)}, u32[]{:S(2)}) collective-permute-start(f32[1,1,16,4,128]{4,3,2,1,0:T(4,128)} %get-tuple-element.78), channel_id=1, source_target_pairs={{0,8},{1,9},{2,10},{3,11},{4,12},{5,13},{6,14},{7,15},{8,16},{9,17... | collective-permute-start | bytes 98312 | tf_op jit(solution)/shard_map/ppermute | solution.py:25
  26.9 252.1 %collective-permute-start.8 = (f32[1,16,16,1,128]{4,3,2,1,0:T(1,128)}, f32[1,16,16,1,128]{4,3,2,1,0:T(1,128)S(1)}, u32[]{:S(2)}, u32[]{:S(2)}) collective-permute-start(f32[1,16,16,1,128]{4,3,2,1,0:T(1,128)} %get-tuple-element.79), channel_id=1, source_target_pairs={{0,64},{64,128},{128,192},{192,256},{256,320},{320,384},{384,448},... | collective-permute-start | bytes 393224 | tf_op jit(solution)/shard_map/ppermute | solution.py:35
  31.6 1.2 copy-start
  32.8 246.2 %copy-start.13 = (f32[16]{0:T(128)}, f32[16]{0:T(128)S(1)}, u32[]{:S(2)}) copy-start(f32[16]{0:T(128)S(1)} %get-tuple-element.96) | copy-start | bytes 196
  35.2 227.9 %copy-start.12 = (f32[1,16,15,4,128]{4,3,2,1,0:T(4,128)S(1)}, f32[1,16,15,4,128]{4,3,2,1,0:T(4,128)}, u32[]{:S(2)}) copy-start(f32[1,16,15,4,128]{4,3,2,1,0:T(4,128)} %get-tuple-element.72) | copy-start | bytes 1474564
  234.0 45.0 %collective-permute-start.9 = (f32[1,16,16,1,128]{4,3,2,1,0:T(1,128)S(1)}, f32[1,16,16,1,128]{4,3,2,1,0:T(1,128)S(1)}, u32[]{:S(2)}, u32[]{:S(2)}) collective-permute-start(f32[1,16,16,1,128]{4,3,2,1,0:T(1,128)S(1)} %get-tuple-element.80), channel_id=1, source_target_pairs={{64,0},{128,64},{192,128},{256,192},{320,256},{384,320},{448,384},... | collective-permute-start | bytes 393224 | tf_op jit(solution)/shard_map/ppermute | solution.py:37
  263.1 1.0 copy-start.10
  263.2 1.2 copy-start.11
  265.0 5.4 collective-permute-start.6
  266.6 0.8 copy-start.3
  267.5 11.6 copy-start.5
  267.5 11.6 copy-start.6
  267.5 11.5 slice-start
  267.6 11.5 copy-start.4
  267.6 11.3 collective-permute-start.2
  269.1 9.9 collective-permute-start.3
  270.4 8.6 collective-permute-start.7
  279.0 0.7 copy-start.16
  279.0 0.7 copy-start.19
  282.1 97.1 %copy-start.1 = (f32[1,16,16,4,128]{4,3,2,1,0:T(4,128)S(1)}, f32[1,16,16,4,128]{4,3,2,1,0:T(4,128)}, u32[]{:S(2)}) copy-start(f32[1,16,16,4,128]{4,3,2,1,0:T(4,128)} %param.6) | copy-start | bytes 1572868
  282.1 116.7 %copy-start.25 = (s32[4,128]{1,0:T(4,128)S(1)}, s32[4,128]{1,0:T(4,128)}, u32[]{:S(2)}) copy-start(s32[4,128]{1,0:T(4,128)} %param.7) | copy-start | bytes 6148
  282.3 64.4 %collective-permute-start.10 = (f32[1,16,16,4,128]{4,3,2,1,0:T(4,128)S(1)}, f32[1,16,16,4,128]{4,3,2,1,0:T(4,128)S(1)}, u32[]{:S(2)}, u32[]{:S(2)}) collective-permute-start(f32[1,16,16,4,128]{4,3,2,1,0:T(4,128)S(1)} %rev.12), channel_id=1, source_target_pairs={{0,1},{1,0},{2,3},{3,2},{4,5},{5,4},{6,7},{7,6},{8,9},{9,8},{10,11... | collective-permute-start | bytes 1572872 | tf_op jit(solution)/shard_map/ppermute | solution.py:51
  346.6 30.7 %collective-permute-start.11 = (f32[1,16,16,4,128]{4,3,2,1,0:T(4,128)S(1)}, f32[1,16,16,4,128]{4,3,2,1,0:T(4,128)S(1)}, u32[]{:S(2)}, u32[]{:S(2)}) collective-permute-start(f32[1,16,16,4,128]{4,3,2,1,0:T(4,128)S(1)} %collective-permute-done.10), channel_id=1, source_target_pairs={{0,2},{2,0},{1,3},{3,1},{4,6},{6,4},{5,7},{7,5},{8,10},{10,8},{9,1... | collective-permute-start | bytes 1572872 | tf_op jit(solution)/shard_map/ppermute | solution.py:51
  377.3 22.5 %collective-permute-start.12 = (f32[1,16,16,4,128]{4,3,2,1,0:T(4,128)S(1)}, f32[1,16,16,4,128]{4,3,2,1,0:T(4,128)S(1)}, u32[]{:S(2)}, u32[]{:S(2)}) collective-permute-start(f32[1,16,16,4,128]{4,3,2,1,0:T(4,128)S(1)} %collective-permute-done.11), channel_id=1, source_target_pairs={{0,4},{4,0},{1,5},{5,1},{2,6},{6,2},{3,7},{7,3},{8,12},{12,8},{9,1... | collective-permute-start | bytes 1572872 | tf_op jit(solution)/shard_map/ppermute | solution.py:51
  379.9 382.9 %collective-permute-start.27 = (f32[1,16,1,4,128]{4,3,2,1,0:T(4,128)}, f32[1,16,1,4,128]{4,3,2,1,0:T(4,128)}, u32[]{:S(2)}, u32[]{:S(2)}) collective-permute-start(f32[1,16,1,4,128]{4,3,2,1,0:T(4,128)} %get-tuple-element.51), channel_id=1, source_target_pairs={{0,1},{1,2},{2,3},{3,4},{4,5},{5,6},{6,7},{7,8},{8,9},{9,10},{10,1... | collective-permute-start | bytes 98312 | tf_op jit(solution)/shard_map/ppermute | solution.py:25
  603.1 12.4 %collective-permute-start.16 = (f32[1,16,1,4,128]{4,3,2,1,0:T(4,128)S(1)}, f32[1,16,1,4,128]{4,3,2,1,0:T(4,128)S(1)}, u32[]{:S(2)}, u32[]{:S(2)}) collective-permute-start(f32[1,16,1,4,128]{4,3,2,1,0:T(4,128)S(1)} %slice.315), channel_id=1, source_target_pairs={{1,0},{2,1},{3,2},{4,3},{5,4},{6,5},{7,6},{8,7},{9,8},{10,9},{11,1... | collective-permute-start | bytes 98312 | tf_op jit(solution)/shard_map/ppermute | solution.py:25
  604.7 52.8 %copy-start.9 = (f32[1,16,16,4,1]{4,3,2,1,0:T(4,128)S(1)}, f32[1,16,16,4,1]{4,3,2,1,0:T(4,128)}, u32[]{:S(2)}) copy-start(f32[1,16,16,4,1]{4,3,2,1,0:T(4,128)} %get-tuple-element.61) | copy-start | bytes 12292
  604.8 52.7 %copy-start.7 = (f32[1,16,16,4,127]{4,3,2,1,0:T(4,128)S(1)}, f32[1,16,16,4,127]{4,3,2,1,0:T(4,128)}, u32[]{:S(2)}) copy-start(f32[1,16,16,4,127]{4,3,2,1,0:T(4,128)} %get-tuple-element.59) | copy-start | bytes 1560580
  604.8 52.7 %copy-start.8 = (f32[1,16,16,4,1]{4,3,2,1,0:T(4,128)S(1)}, f32[1,16,16,4,1]{4,3,2,1,0:T(4,128)}, u32[]{:S(2)}) copy-start(f32[1,16,16,4,1]{4,3,2,1,0:T(4,128)} %get-tuple-element.60) | copy-start | bytes 12292
  604.9 12.6 %collective-permute-start.15 = (f32[1,16,1,4,128]{4,3,2,1,0:T(4,128)S(1)}, f32[1,16,1,4,128]{4,3,2,1,0:T(4,128)S(1)}, u32[]{:S(2)}, u32[]{:S(2)}) collective-permute-start(f32[1,16,1,4,128]{4,3,2,1,0:T(4,128)S(1)} %slice.312), channel_id=1, source_target_pairs={{0,1},{1,2},{2,3},{3,4},{4,5},{5,6},{6,7},{7,8},{8,9},{9,10},{10,1... | collective-permute-start | bytes 98312 | tf_op jit(solution)/shard_map/ppermute | solution.py:25
  612.9 35.9 %collective-permute-start.13 = (f32[1,1,16,4,128]{4,3,2,1,0:T(4,128)S(1)}, f32[1,1,16,4,128]{4,3,2,1,0:T(4,128)S(1)}, u32[]{:S(2)}, u32[]{:S(2)}) collective-permute-start(f32[1,1,16,4,128]{4,3,2,1,0:T(4,128)S(1)} %slice.308), channel_id=1, source_target_pairs={{0,8},{1,9},{2,10},{3,11},{4,12},{5,13},{6,14},{7,15},{8,16},{9,17... | collective-permute-start | bytes 98312 | tf_op jit(solution)/shard_map/ppermute | solution.py:25
  614.2 35.9 %collective-permute-start.14 = (f32[1,1,16,4,128]{4,3,2,1,0:T(4,128)S(1)}, f32[1,1,16,4,128]{4,3,2,1,0:T(4,128)S(1)}, u32[]{:S(2)}, u32[]{:S(2)}) collective-permute-start(f32[1,1,16,4,128]{4,3,2,1,0:T(4,128)S(1)} %slice.311), channel_id=1, source_target_pairs={{8,0},{9,1},{10,2},{11,3},{12,4},{13,5},{14,6},{15,7},{16,8},{17,9... | collective-permute-start | bytes 98312 | tf_op jit(solution)/shard_map/ppermute | solution.py:25
  615.5 40.0 %collective-permute-start.17 = (f32[1,16,16,1,128]{4,3,2,1,0:T(1,128)S(1)}, f32[1,16,16,1,128]{4,3,2,1,0:T(1,128)S(1)}, u32[]{:S(2)}, u32[]{:S(2)}) collective-permute-start(f32[1,16,16,1,128]{4,3,2,1,0:T(1,128)S(1)} %get-tuple-element.64), channel_id=1, source_target_pairs={{0,64},{64,128},{128,192},{192,256},{256,320},{320,384},{384,448},... | collective-permute-start | bytes 393224 | tf_op jit(solution)/shard_map/ppermute | solution.py:35
  617.5 39.9 %collective-permute-start.18 = (f32[1,16,16,1,128]{4,3,2,1,0:T(1,128)S(1)}, f32[1,16,16,1,128]{4,3,2,1,0:T(1,128)S(1)}, u32[]{:S(2)}, u32[]{:S(2)}) collective-permute-start(f32[1,16,16,1,128]{4,3,2,1,0:T(1,128)S(1)} %get-tuple-element.65), channel_id=1, source_target_pairs={{64,0},{128,64},{192,128},{256,192},{320,256},{384,320},{448,384},... | collective-permute-start | bytes 393224 | tf_op jit(solution)/shard_map/ppermute | solution.py:37
  648.8 115.3 %collective-permute-start.26 = (f32[1,16,1,4,128]{4,3,2,1,0:T(4,128)}, f32[1,16,1,4,128]{4,3,2,1,0:T(4,128)}, u32[]{:S(2)}, u32[]{:S(2)}) collective-permute-start(f32[1,16,1,4,128]{4,3,2,1,0:T(4,128)} %get-tuple-element.50), channel_id=1, source_target_pairs={{1,0},{2,1},{3,2},{4,3},{5,4},{6,5},{7,6},{8,7},{9,8},{10,9},{11,1... | collective-permute-start | bytes 98312 | tf_op jit(solution)/shard_map/ppermute | solution.py:25
  650.1 328.6 %collective-permute-start.22 = (f32[1,16,16,1,128]{4,3,2,1,0:T(1,128)}, f32[1,16,16,1,128]{4,3,2,1,0:T(1,128)S(1)}, u32[]{:S(2)}, u32[]{:S(2)}) collective-permute-start(f32[1,16,16,1,128]{4,3,2,1,0:T(1,128)} %get-tuple-element.56), channel_id=1, source_target_pairs={{64,0},{128,64},{192,128},{256,192},{320,256},{384,320},{448,384},... | collective-permute-start | bytes 393224 | tf_op jit(solution)/shard_map/ppermute | solution.py:37
  655.5 323.2 %collective-permute-start.23 = (f32[1,16,16,1,128]{4,3,2,1,0:T(1,128)}, f32[1,16,16,1,128]{4,3,2,1,0:T(1,128)S(1)}, u32[]{:S(2)}, u32[]{:S(2)}) collective-permute-start(f32[1,16,16,1,128]{4,3,2,1,0:T(1,128)} %get-tuple-element.57), channel_id=1, source_target_pairs={{0,64},{64,128},{128,192},{192,256},{256,320},{320,384},{384,448},... | collective-permute-start | bytes 393224 | tf_op jit(solution)/shard_map/ppermute | solution.py:35
  657.5 0.7 copy-start.17
  657.5 0.7 copy-start.20
  660.7 53.1 %collective-permute-start.19 = (f32[1,16,16,4,128]{4,3,2,1,0:T(4,128)S(1)}, f32[1,16,16,4,128]{4,3,2,1,0:T(4,128)S(1)}, u32[]{:S(2)}, u32[]{:S(2)}) collective-permute-start(f32[1,16,16,4,128]{4,3,2,1,0:T(4,128)S(1)} %rev.13), channel_id=1, source_target_pairs={{0,1},{1,0},{2,3},{3,2},{4,5},{5,4},{6,7},{7,6},{8,9},{9,8},{10,11... | collective-permute-start | bytes 1572872 | tf_op jit(solution)/shard_map/ppermute | solution.py:51
  713.8 36.3 %collective-permute-start.20 = (f32[1,16,16,4,128]{4,3,2,1,0:T(4,128)S(1)}, f32[1,16,16,4,128]{4,3,2,1,0:T(4,128)S(1)}, u32[]{:S(2)}, u32[]{:S(2)}) collective-permute-start(f32[1,16,16,4,128]{4,3,2,1,0:T(4,128)S(1)} %collective-permute-done.19), channel_id=1, source_target_pairs={{0,2},{2,0},{1,3},{3,1},{4,6},{6,4},{5,7},{7,5},{8,10},{10,8},{9,1... | collective-permute-start | bytes 1572872 | tf_op jit(solution)/shard_map/ppermute | solution.py:51
  750.1 22.8 %collective-permute-start.21 = (f32[1,16,16,4,128]{4,3,2,1,0:T(4,128)S(1)}, f32[1,16,16,4,128]{4,3,2,1,0:T(4,128)S(1)}, u32[]{:S(2)}, u32[]{:S(2)}) collective-permute-start(f32[1,16,16,4,128]{4,3,2,1,0:T(4,128)S(1)} %collective-permute-done.20), channel_id=1, source_target_pairs={{0,4},{4,0},{1,5},{5,1},{2,6},{6,2},{3,7},{7,3},{8,12},{12,8},{9,1... | collective-permute-start | bytes 1572872 | tf_op jit(solution)/shard_map/ppermute | solution.py:51
  762.8 215.9 %collective-permute-start.24 = (f32[1,1,16,4,128]{4,3,2,1,0:T(4,128)}, f32[1,1,16,4,128]{4,3,2,1,0:T(4,128)}, u32[]{:S(2)}, u32[]{:S(2)}) collective-permute-start(f32[1,1,16,4,128]{4,3,2,1,0:T(4,128)} %get-tuple-element.46), channel_id=1, source_target_pairs={{8,0},{9,1},{10,2},{11,3},{12,4},{13,5},{14,6},{15,7},{16,8},{17,9... | collective-permute-start | bytes 98312 | tf_op jit(solution)/shard_map/ppermute | solution.py:25
  764.1 214.6 %collective-permute-start.25 = (f32[1,1,16,4,128]{4,3,2,1,0:T(4,128)}, f32[1,1,16,4,128]{4,3,2,1,0:T(4,128)}, u32[]{:S(2)}, u32[]{:S(2)}) collective-permute-start(f32[1,1,16,4,128]{4,3,2,1,0:T(4,128)} %get-tuple-element.47), channel_id=1, source_target_pairs={{0,8},{1,9},{2,10},{3,11},{4,12},{5,13},{6,14},{7,15},{8,16},{9,17... | collective-permute-start | bytes 98312 | tf_op jit(solution)/shard_map/ppermute | solution.py:25
  774.7 0.7 copy-start.23
  774.7 0.7 copy-start.22
  978.7 0.7 copy-start.18
  978.7 0.7 copy-start.21
  983.2 17.4 %collective-permute-start.28 = (f32[1,16,16,4,128]{4,3,2,1,0:T(4,128)S(1)}, f32[1,16,16,4,128]{4,3,2,1,0:T(4,128)S(1)}, u32[]{:S(2)}, u32[]{:S(2)}) collective-permute-start(f32[1,16,16,4,128]{4,3,2,1,0:T(4,128)S(1)} %rev.14), channel_id=1, source_target_pairs={{0,1},{1,0},{2,3},{3,2},{4,5},{5,4},{6,7},{7,6},{8,9},{9,8},{10,11... | collective-permute-start | bytes 1572872 | tf_op jit(solution)/shard_map/ppermute | solution.py:51
  1000.5 24.0 %collective-permute-start.29 = (f32[1,16,16,4,128]{4,3,2,1,0:T(4,128)S(1)}, f32[1,16,16,4,128]{4,3,2,1,0:T(4,128)S(1)}, u32[]{:S(2)}, u32[]{:S(2)}) collective-permute-start(f32[1,16,16,4,128]{4,3,2,1,0:T(4,128)S(1)} %collective-permute-done.28), channel_id=1, source_target_pairs={{0,2},{2,0},{1,3},{3,1},{4,6},{6,4},{5,7},{7,5},{8,10},{10,8},{9,1... | collective-permute-start | bytes 1572872 | tf_op jit(solution)/shard_map/ppermute | solution.py:51
  1024.5 19.4 %collective-permute-start.30 = (f32[1,16,16,4,128]{4,3,2,1,0:T(4,128)S(1)}, f32[1,16,16,4,128]{4,3,2,1,0:T(4,128)S(1)}, u32[]{:S(2)}, u32[]{:S(2)}) collective-permute-start(f32[1,16,16,4,128]{4,3,2,1,0:T(4,128)S(1)} %collective-permute-done.29), channel_id=1, source_target_pairs={{0,4},{4,0},{1,5},{5,1},{2,6},{6,2},{3,7},{7,3},{8,12},{12,8},{9,1... | collective-permute-start | bytes 1572872 | tf_op jit(solution)/shard_map/ppermute | solution.py:51
  1045.4 55.8 %collective-permute-start.36 = (f32[1,16,1,4,128]{4,3,2,1,0:T(4,128)S(1)}, f32[1,16,1,4,128]{4,3,2,1,0:T(4,128)S(1)}, u32[]{:S(2)}, u32[]{:S(2)}) collective-permute-start(f32[1,16,1,4,128]{4,3,2,1,0:T(4,128)S(1)} %get-tuple-element.37), channel_id=1, source_target_pairs={{0,1},{1,2},{2,3},{3,4},{4,5},{5,6},{6,7},{7,8},{8,9},{9,10},{10,1... | collective-permute-start | bytes 98312 | tf_op jit(solution)/shard_map/ppermute | solution.py:25
  1046.7 61.7 %collective-permute-start.31 = (f32[1,16,16,1,128]{4,3,2,1,0:T(1,128)S(1)}, f32[1,16,16,1,128]{4,3,2,1,0:T(1,128)S(1)}, u32[]{:S(2)}, u32[]{:S(2)}) collective-permute-start(f32[1,16,16,1,128]{4,3,2,1,0:T(1,128)S(1)} %get-tuple-element.42), channel_id=1, source_target_pairs={{64,0},{128,64},{192,128},{256,192},{320,256},{384,320},{448,384},... | collective-permute-start | bytes 393224 | tf_op jit(solution)/shard_map/ppermute | solution.py:37
  1096.7 11.7 collective-permute-start.32
  1098.6 9.7 collective-permute-start.35
  1099.9 8.5 collective-permute-start.33
  1101.2 7.2 collective-permute-start.34
  1111.6 45.6 %collective-permute-start.37 = (f32[1,16,16,4,128]{4,3,2,1,0:T(4,128)S(1)}, f32[1,16,16,4,128]{4,3,2,1,0:T(4,128)S(1)}, u32[]{:S(2)}, u32[]{:S(2)}) collective-permute-start(f32[1,16,16,4,128]{4,3,2,1,0:T(4,128)S(1)} %rev.15), channel_id=1, source_target_pairs={{0,1},{1,0},{2,3},{3,2},{4,5},{5,4},{6,7},{7,6},{8,9},{9,8},{10,11... | collective-permute-start | bytes 1572872 | tf_op jit(solution)/shard_map/ppermute | solution.py:51
  1157.1 34.1 %collective-permute-start.38 = (f32[1,16,16,4,128]{4,3,2,1,0:T(4,128)S(1)}, f32[1,16,16,4,128]{4,3,2,1,0:T(4,128)S(1)}, u32[]{:S(2)}, u32[]{:S(2)}) collective-permute-start(f32[1,16,16,4,128]{4,3,2,1,0:T(4,128)S(1)} %collective-permute-done.37), channel_id=1, source_target_pairs={{0,2},{2,0},{1,3},{3,1},{4,6},{6,4},{5,7},{7,5},{8,10},{10,8},{9,1... | collective-permute-start | bytes 1572872 | tf_op jit(solution)/shard_map/ppermute | solution.py:51
  1191.3 22.9 %collective-permute-start.39 = (f32[1,16,16,4,128]{4,3,2,1,0:T(4,128)S(1)}, f32[1,16,16,4,128]{4,3,2,1,0:T(4,128)S(1)}, u32[]{:S(2)}, u32[]{:S(2)}) collective-permute-start(f32[1,16,16,4,128]{4,3,2,1,0:T(4,128)S(1)} %collective-permute-done.38), channel_id=1, source_target_pairs={{0,4},{4,0},{1,5},{5,1},{2,6},{6,2},{3,7},{7,3},{8,12},{12,8},{9,1... | collective-permute-start | bytes 1572872 | tf_op jit(solution)/shard_map/ppermute | solution.py:51
  (3 other events, 1.9 us)
where the time goes:
time: 1230 us; the launch traced here: 1220 us
  blocking collectives  599 us (49%)
  starting transfers between devices  317 us (26%)
  waiting for transfers between devices  252 us (20%)
  local copies, waits for them, and re-layouts  24.3 us (2%)
  other arithmetic  19.6 us (2%)
    psum x3, blocking collectives, moment_stats(): total, mom_x, mom_y = lax.psum((total, mom_x, mom_y), 'vert')  599 us
    ppermute x12, waiting for transfers between devices, partner_2(): return lax.ppermute(block, axis, route)  243 us
    ppermute x12, starting transfers between devices, partner_2(): return lax.ppermute(block, axis, route)  116 us
    ppermute x4, starting transfers between devices, with_halo(): lax.ppermute(head, axis, [((i + 1) % count, i) for i in range(count)])  116 us
    ppermute x20, starting transfers between devices, from_behind(): return lax.ppermute(x, axis, pairs)  76 us
  transfers between devices with their start and end apart: 40, of which 13 were waited for; matrix products, arithmetic and copies ran while one was open for 2% of the time, Pallas kernels for 0%

commit v1 on v0

v1 whole, which is shorter than its diff:
```python
import functools

import jax
import jax.numpy as jnp
from jax import lax
from jax.experimental import pallas as pl
from jax.experimental.pallas import tpu as pltpu
from jax.sharding import PartitionSpec as P

MESH = pl.DeviceIdType.MESH
F32 = jnp.float32

VX = 128
VY = 128
KX = 8
KY = 8
BX = 16
BY = 16
TILES = 8
PACK = 4

advect_rate = 0.3
diffusion = 0.05
drift_limit = 0.1
hamilton_rate = 0.05
time_step = 0.2
density_cost = 2.0
velocity_cost = 1.0


def roll4(a):
    return pltpu.roll(a, 4, axis=a.ndim - 2)


def kernel(
    m_ref, g_ref, u_ref, walls_ref, mo_ref, vo_ref,
    mext, mext2, gext, gradx, grady, gradh, upx, dnx, field, uext, vext, pre, wz,
    hy, xh, ylo, yhi, ysend, xsend, gvy, csend, crecv, red, tiles, idx,
    send_sem, recv_sem,
):
    vert = lax.axis_index("vert")
    gx = lax.axis_index("gx")
    gx_count = lax.axis_size("gx")
    i = vert // KY
    j = vert % KY
    zh = vert % 4
    px = (vert // 4) % 4
    py = vert // 16

    def at(y, x, z):
        return {"vert": ((y % 4) * 4 + x % 4) * 4 + z % 4}

    plane = [at(py + d // 4, px + d % 4, zh) for d in range(1, 16)]
    depth = [at(py, px, zh + d) for d in range(1, 4)]
    mirror = {"vert": i * KY + (KY - 1 - j)}
    vx_up = {"vert": ((i + 1) % KX) * KY + j}
    vx_down = {"vert": ((i + KX - 1) % KX) * KY + j}
    vy_up = {"vert": i * KY + (j + 1) % KY}
    vy_down = {"vert": i * KY + (j + KY - 1) % KY}
    x_up = {"gx": (gx + 1) % gx_count}
    x_down = {"gx": (gx + gx_count - 1) % gx_count}

    barrier = pltpu.get_barrier_semaphore()
    roles = plane + depth + [mirror, vy_up, vy_down, x_up, x_down]
    for peer in roles:
        pl.semaphore_signal(barrier, inc=1, device_id=peer, device_id_type=MESH)

    row = lax.broadcasted_iota(jnp.int32, (8, 128), 0)
    lane = lax.broadcasted_iota(jnp.int32, (8, 128), 1)
    lo8 = row < 4
    high_x = i >= KX // 2
    high_y = j >= KY // 2

    def vx_hat(e):
        return ((i * BX + e).astype(F32) - (VX - 1) / 2.0) / (VX / 2.0)

    shape = (TILES, 8, 128)
    vy_row = 2 * lax.broadcasted_iota(jnp.int32, shape, 0) + lax.broadcasted_iota(jnp.int32, shape, 1) // 4
    vy_hat = ((j * BY + vy_row).astype(F32) - (VY - 1) / 2.0) / (VY / 2.0)
    vy_edge = jnp.where(lo8, j * BY - 1, j * BY + BY)
    vy_hat_edge = (vy_edge.astype(F32) - (VY - 1) / 2.0) / (VY / 2.0)
    inside_edge = (vy_edge >= 0) & (vy_edge < VY)
    speed_y = jnp.abs(advect_rate * vy_hat)

    def local_moments(read):
        def body(vx, carry):
            total, mom_x, mom_y = carry
            slab = read(vx)
            s = jnp.sum(slab, axis=0)
            return (total + s, mom_x + vx_hat(vx) * s, mom_y + jnp.sum(vy_hat * slab, axis=0))

        zero = jnp.zeros((8, 128), F32)
        return lax.fori_loop(0, BX, body, (zero, zero, zero))

    def put_moments(slot, sums):
        total, mom_x, mom_y = (a + roll4(a) for a in sums)
        red[slot, 0] = jnp.where(lo8, total, mom_x)
        red[slot, 1] = mom_y

    put_moments(0, local_moments(lambda vx: m_ref[vx]))

    w4 = walls_ref[...]
    wall = jnp.concatenate([w4, w4], axis=0) == 1
    ones = wall.astype(F32)
    sub128 = lax.broadcasted_iota(jnp.int32, (128, 128), 0)
    lane128 = lax.broadcasted_iota(jnp.int32, (128, 128), 1)
    upto = (sub128 <= lane128).astype(F32)
    count = jnp.dot(ones, upto, preferred_element_type=F32)
    count_t = lax.dot_general(
        (lane128 <= sub128).astype(F32), ones, (((1,), (1,)), ((), ())), preferred_element_type=F32
    )
    rank = jnp.clip(count.astype(jnp.int32) - 1, 0, 31)
    nth = (lane128 % 32).astype(F32)
    pick = jnp.zeros((8, 128), F32)
    for x in range(4):
        place = jnp.sum((count_t[:, x : x + 1] <= nth).astype(F32), axis=0, keepdims=True)
        pick = jnp.where(row % 4 == x, place, pick)
    idx[0] = jnp.minimum(pick.astype(jnp.int32), 127)
    idx[1] = rank

    def along_y(slab, index):
        return jnp.take_along_axis(slab, jnp.broadcast_to(index[None], shape), axis=2)

    pl.semaphore_wait(barrier, len(roles))

    counter = [0]

    def copy(src, dst, peer):
        n = counter[0]
        counter[0] += 1
        return pltpu.make_async_remote_copy(
            src_ref=src, dst_ref=dst, send_sem=send_sem.at[n], recv_sem=recv_sem.at[n],
            device_id=peer, device_id_type=MESH,
        )

    sent = []

    def start(src, dst, peer):
        c = copy(src, dst, peer)
        c.start()
        sent.append(c)
        return c

    def arrive(copies):
        for c in copies:
            c.wait_recv()

    def plane_start(r):
        base = 20 * r
        return [start(red.at[base], red.at[base + 1 + d], peer) for d, peer in enumerate(plane)]

    def plane_finish(r, copies):
        base = 20 * r
        arrive(copies)
        acc = red[base]
        for d in range(15):
            acc = acc + red[base + 1 + d]
        red[base + 16] = acc
        return [start(red.at[base + 16], red.at[base + 17 + d], peer) for d, peer in enumerate(depth)]

    def depth_finish(r, copies, reflected):
        base = 20 * r
        arrive(copies)
        acc = red[base + 16]
        for d in range(3):
            acc = acc + red[base + 17 + d]
        swapped = roll4(acc[0])
        total = jnp.where(lo8, acc[0], swapped)
        mom_x = jnp.where(lo8, swapped, acc[0])
        mean_y = acc[1] / total
        if reflected:
            mean_y = jnp.where(wall, 0.0, mean_y)
        return total, mom_x / total, mean_y

    def vy_faces(slot, read):
        def body(p, _):
            a0, a1 = read(2 * p, TILES - 1), read(2 * p + 1, TILES - 1)
            ysend[slot, p] = jnp.where(lo8, roll4(a0), a1)
            b0, b1 = read(2 * p, 0), read(2 * p + 1, 0)
            ysend[slot + 1, p] = jnp.where(lo8, b0, roll4(b1))
            return 0

        lax.fori_loop(0, BX // 2, body, 0)
        return [
            start(ysend.at[slot], ylo.at[slot // 2], vy_up),
            start(ysend.at[slot + 1], yhi.at[slot // 2], vy_down),
        ]

    def vy_halo(slot, copies):
        arrive(copies)

        def body(p, _):
            low, high = ylo[slot // 2, p], yhi[slot // 2, p]
            hy[slot // 2, 2 * p] = jnp.where(inside_edge, jnp.where(lo8, low, roll4(high)), 0.0)
            hy[slot // 2, 2 * p + 1] = jnp.where(inside_edge, jnp.where(lo8, roll4(low), high), 0.0)
            return 0

        lax.fori_loop(0, BX // 2, body, 0)

    def vx_faces(ext):
        return [
            start(ext.at[BX], ext.at[0], vx_up),
            start(ext.at[1], ext.at[BX + 1], vx_down),
        ]

    def vx_halo(ext, copies):
        arrive(copies)
        ext[0] = jnp.where(i == 0, 0.0, ext[0])
        ext[BX + 1] = jnp.where(i == KX - 1, 0.0, ext[BX + 1])

    def x_faces(slot, read, below):
        def body(q, _):
            face = None
            for b in range(PACK):
                slab = read(PACK * q + b)
                moved = jnp.where(below, pltpu.roll(slab, (b - 3) % 8, axis=1), pltpu.roll(slab, (b + 3) % 8, axis=1))
                target = jnp.where(below, b, b + 3) % 4
                face = moved if face is None else jnp.where((row % 4 == target)[None], moved, face)
            xsend[slot, q] = face
            return 0

        lax.fori_loop(0, BX // PACK, body, 0)

    def x_neighbour(slab, slot, q, b, below):
        shifted = jnp.where(below, pltpu.roll(slab, 1, axis=1), pltpu.roll(slab, 7, axis=1))
        edge = row % 4 == jnp.where(below, 0, 3)
        return jnp.where(edge[None], pltpu.roll(xh[slot, q], (8 - b) % 8, axis=1), shifted)

    def y_neighbour(slab, below):
        return pltpu.roll(slab, jnp.where(below, 1, 127), axis=2)

    def vy_neighbours(low, high, edge_low, edge_high):
        r_low, r_high = roll4(low), roll4(high)
        lower = jnp.where(lo8[None], jnp.concatenate([edge_low[None], r_low[:-1]], axis=0), r_low)
        upper = jnp.where(lo8[None], r_high, jnp.concatenate([r_high[1:], edge_high[None]], axis=0))
        return lower, upper

    def both_vy(slab, edge):
        r = roll4(slab)
        lower = jnp.where(lo8[None], jnp.concatenate([edge[None], r[:-1]], axis=0), r)
        upper = jnp.where(lo8[None], r, jnp.concatenate([r[1:], edge[None]], axis=0))
        return lower, upper

    def mirror_copies(slot):
        n = counter[0]
        counter[0] += PACK

        def make(q):
            return pltpu.make_async_remote_copy(
                src_ref=csend.at[slot, q], dst_ref=crecv.at[slot, q],
                send_sem=send_sem.at[n + q], recv_sem=recv_sem.at[n + q],
                device_id=mirror, device_id_type=MESH,
            )

        return make

    def packed(face, slab, b):
        taken = along_y(slab, idx[0])
        return taken if face is None else jnp.where((lane // 32 == b)[None], taken, face)

    def send_packed(slot, q, face, make):
        turned = roll4(face)
        for t in range(TILES):
            csend[slot, q, t] = turned[TILES - 1 - t]
        make(q).start()

    def reflect(slot, make, read, write):
        def body(q, carry):
            make(q).wait_recv()
            face = crecv[slot, q]
            for b in range(PACK):
                vx = PACK * q + b
                slab = read(vx)
                other = along_y(face, idx[1] + 32 * b)
                write(vx, jnp.where(wall[None], 0.5 * (slab + other), slab))
            return carry

        lax.fori_loop(0, PACK, body, 0)

    def forward(ext, slot, xslot, stats, write, cslot):
        total, mean_x, mean_y = stats

        def rates(e, _):
            cells = ext[e]
            drift = drift_limit * jnp.tanh((mean_x - vx_hat(e - 1))[None] - gradx[e])
            upx[e] = cells * (diffusion + jnp.maximum(drift, 0.0))
            dnx[e] = cells * (diffusion + jnp.maximum(-drift, 0.0))
            return 0

        lax.fori_loop(0, BX + 2, rates, 0)
        make = mirror_copies(cslot)

        def body(q, carry):
            total, mom_x, mom_y = carry
            face = None
            for b in range(PACK):
                vx = PACK * q + b
                cells = ext[vx + 1]
                drift = drift_limit * jnp.tanh(mean_y[None] - vy_hat - grady[vx])
                up = cells * (diffusion + jnp.maximum(drift, 0.0))
                down = cells * (diffusion + jnp.maximum(-drift, 0.0))
                drift_e = drift_limit * jnp.tanh(mean_y - vy_hat_edge - gradh[vx])
                cells_e = hy[slot // 2, vx]
                up_e = cells_e * (diffusion + jnp.maximum(drift_e, 0.0))
                down_e = cells_e * (diffusion + jnp.maximum(-drift_e, 0.0))
                lower, upper = vy_neighbours(up, down, up_e, down_e)
                flow = upx[vx] + dnx[vx + 2] + lower + upper - (upx[vx + 1] + dnx[vx + 1] + up + down)
                speed_x = jnp.abs(advect_rate * vx_hat(vx))
                moved = speed_x * (cells - x_neighbour(cells, xslot, q, b, high_x))
                moved = moved + speed_y * (cells - y_neighbour(cells, high_y))
                new = cells + flow - moved
                write(vx, new)
                s = jnp.sum(new, axis=0)
                total = total + s
                mom_x = mom_x + vx_hat(vx) * s
                mom_y = mom_y + jnp.sum(vy_hat * new, axis=0)
                face = packed(face, new, b)
            send_packed(cslot, q, face, make)
            return total, mom_x, mom_y

        zero = jnp.zeros((8, 128), F32)
        sums = lax.fori_loop(0, PACK, body, (zero, zero, zero))
        return sums, make

    plane0 = plane_start(0)

    def fill(ext, ref, lead):
        def body(vx, _):
            ext[vx + lead] = ref[vx]
            return 0

        lax.fori_loop(0, BX, body, 0)

    fill(uext, u_ref, 1)
    u_vx = vx_faces(uext)
    u_vy = vy_faces(0, lambda vx, t: u_ref[vx, t])
    x_faces(0, lambda vx: u_ref[vx], jnp.logical_not(high_x))

    def x_send(slot, below):
        peer = {"gx": jnp.where(below, (gx + 1) % gx_count, (gx + gx_count - 1) % gx_count)}
        return start(xsend.at[slot], xh.at[slot], peer)

    u_x = x_send(0, jnp.logical_not(high_x))
    fill(gext, g_ref, 2)
    g_vx = [
        start(gext.at[pl.ds(BX, 2)], gext.at[pl.ds(0, 2)], vx_up),
        start(gext.at[pl.ds(2, 2)], gext.at[pl.ds(BX + 2, 2)], vx_down),
    ]
    fill(mext, m_ref, 1)
    m_vx = vx_faces(mext)
    m_vy = vy_faces(2, lambda vx, t: m_ref[vx, t])
    x_faces(1, lambda vx: m_ref[vx], high_x)
    m_x = x_send(1, high_x)

    def fill_g(vx, _):
        gvy[0, vx] = g_ref[vx, TILES - 1]
        gvy[1, vx] = g_ref[vx, 0]
        return 0

    lax.fori_loop(0, BX, fill_g, 0)
    g_vy = [start(gvy.at[0], gvy.at[2], vy_up), start(gvy.at[1], gvy.at[3], vy_down)]

    depth0 = plane_finish(0, plane0)

    vx_halo(uext, u_vx)
    vy_halo(0, u_vy)
    arrive([u_x])
    make_u = mirror_copies(0)

    def value_step(q, _):
        face = None
        for b in range(PACK):
            vx = PACK * q + b
            below, here, above = uext[vx], uext[vx + 1], uext[vx + 2]
            lower, upper = both_vy(here, hy[0, vx])
            grad_x = 0.5 * (above - below)
            grad_y = 0.5 * (upper - lower)
            laplace = above + below + upper + lower - 4.0 * here
            speed_x = jnp.abs(advect_rate * vx_hat(vx))
            moved = speed_x * (x_neighbour(here, 0, q, b, jnp.logical_not(high_x)) - here)
            moved = moved + speed_y * (y_neighbour(here, jnp.logical_not(high_y)) - here)
            new = here + moved - hamilton_rate * (grad_x * grad_x + grad_y * grad_y) + diffusion * laplace
            pre[vx] = new
            face = packed(face, new, b)
        send_packed(0, q, face, make_u)
        return 0

    lax.fori_loop(0, PACK, value_step, 0)

    arrive(g_vx)
    for s in range(2):
        gext[s] = jnp.where(i == 0, 0.0, gext[s])
        gext[BX + 2 + s] = jnp.where(i == KX - 1, 0.0, gext[BX + 2 + s])

    def grads_x(e, _):
        gradx[e] = 0.5 * (gext[e + 2] - gext[e])
        return 0

    lax.fori_loop(0, BX + 2, grads_x, 0)
    arrive(g_vy)

    def grads_y(vx, _):
        low = jnp.where(j == 0, 0.0, gvy[2, vx])
        high = jnp.where(j == KY - 1, 0.0, gvy[3, vx])
        slab = gext[vx + 2]
        edge = jnp.where(lo8, roll4(low), roll4(high))
        lower, upper = both_vy(slab, edge)
        grady[vx] = 0.5 * (upper - lower)
        gradh[vx] = jnp.where(lo8, 0.5 * (slab[0] - low), 0.5 * (high - slab[TILES - 1]))
        return 0

    lax.fori_loop(0, BX, grads_y, 0)

    vx_halo(mext, m_vx)
    vy_halo(2, m_vy)
    arrive([m_x])
    stats0 = depth_finish(0, depth0, False)

    def write_field(vx, slab):
        field[vx] = slab

    sums1, make_1 = forward(mext, 2, 1, stats0, write_field, 1)
    put_moments(20, sums1)
    plane1 = plane_start(1)

    def write_v(vx, slab):
        vext[vx + 1] = slab

    reflect(0, make_u, lambda vx: pre[vx], write_v)
    v_vx = vx_faces(vext)
    x_faces(2, lambda vx: vext[vx + 1], jnp.logical_not(high_x))
    v_x = x_send(2, jnp.logical_not(high_x))
    depth1 = plane_finish(1, plane1)

    def write_m(vx, slab):
        mext2[vx + 1] = slab

    reflect(1, make_1, lambda vx: field[vx], write_m)
    n_vx = vx_faces(mext2)
    n_vy = vy_faces(4, lambda vx, t: mext2[vx + 1, t])
    x_faces(3, lambda vx: mext2[vx + 1], high_x)
    n_x = x_send(3, high_x)

    arrive([v_x])
    make_z = mirror_copies(2)

    def transport_step(q, _):
        face = None
        for b in range(PACK):
            vx = PACK * q + b
            here = vext[vx + 1]
            speed_x = jnp.abs(advect_rate * vx_hat(vx))
            moved = speed_x * x_neighbour(here, 2, q, b, jnp.logical_not(high_x))
            moved = moved + speed_y * y_neighbour(here, jnp.logical_not(high_y))
            pre[vx] = moved
            face = packed(face, moved, b)
        send_packed(2, q, face, make_z)
        return 0

    lax.fori_loop(0, PACK, transport_step, 0)
    v_vy = vy_faces(6, lambda vx, t: vext[vx + 1, t])

    stats1 = depth_finish(1, depth1, True)
    vx_halo(mext2, n_vx)
    vy_halo(4, n_vy)
    arrive([n_x])

    def write_out(vx, slab):
        mo_ref[vx] = slab

    sums2, make_2 = forward(mext2, 4, 3, stats1, write_out, 3)
    put_moments(40, sums2)
    plane2 = plane_start(2)

    def write_z(vx, slab):
        wz[vx] = slab

    vx_halo(vext, v_vx)
    vy_halo(6, v_vy)
    depth2 = plane_finish(2, plane2)
    reflect(2, make_z, lambda vx: pre[vx], write_z)
    total2, mean_x2, mean_y2 = depth_finish(2, depth2, True)

    half = 0.5 * time_step * velocity_cost

    def coefficients(total, mean_x, mean_y):
        density = time_step * density_cost * (total / (VX * VY))
        return density + half * (mean_x * mean_x + mean_y * mean_y), 2.0 * half * mean_x, 2.0 * half * mean_y

    c0, c1, c2 = coefficients(total2, mean_x2, mean_y2)
    e0, e1, e2 = coefficients(*stats1)
    tiles[0] = c0
    tiles[1] = c1
    tiles[2] = c2
    back = jnp.logical_not(high_x)
    stats_peer = {"gx": jnp.where(back, (gx + 1) % gx_count, (gx + gx_count - 1) % gx_count)}
    stats_copy = start(tiles.at[pl.ds(0, 3)], tiles.at[pl.ds(3, 3)], stats_peer)

    def write_end(vx, slab):
        mo_ref[vx] = slab

    reflect(3, make_2, lambda vx: mo_ref[vx], write_end)
    arrive([stats_copy])

    def x_tile(t):
        here = tiles[t]
        shifted = jnp.where(back, pltpu.roll(here, 1, axis=0), pltpu.roll(here, 7, axis=0))
        far = jnp.where(back, pltpu.roll(tiles[3 + t], 5, axis=0), pltpu.roll(tiles[3 + t], 3, axis=0))
        return jnp.where(row % 4 == jnp.where(back, 0, 3), far, shifted)

    down_y = jnp.logical_not(high_y)
    near = jnp.where(down_y, 1, 127)
    away = jnp.where(down_y, 127, 1)
    y_near = [pltpu.roll(c, near, axis=1) for c in (c0, c1, c2)]
    y_away = [pltpu.roll(c, away, axis=1) for c in (c0, c1, c2)]
    x0, x1, x2 = x_tile(0), x_tile(1), jnp.where(wall, 0.0, x_tile(2))
    y0 = jnp.where(wall, 0.5 * (y_near[0] + y_away[0]), y_near[0])
    y1 = jnp.where(wall, 0.5 * (y_near[1] + y_away[1]), y_near[1])
    y2 = jnp.where(wall, 0.5 * (y_near[2] - y_away[2]), y_near[2])

    def cost(k0, k1, k2, vxh, vyh):
        return k0 - k1 * vxh - k2 * vyh + half * (vxh * vxh + vyh * vyh)

    def last_step(vx, _):
        vxh, vxh_low, vxh_high = vx_hat(vx), vx_hat(vx - 1), vx_hat(vx + 1)
        run_v = half * vy_hat * vy_hat - c2[None] * vy_hat + c0[None]
        run = (half * vxh * vxh - c1 * vxh)[None] + run_v
        has_low = (i * BX + vx) > 0
        has_high = (i * BX + vx) < VX - 1
        here = vext[vx + 1] + run
        below = vext[vx] + jnp.where(has_low, (half * vxh_low * vxh_low - c1 * vxh_low)[None] + run_v, 0.0)
        above = vext[vx + 2] + jnp.where(has_high, (half * vxh_high * vxh_high - c1 * vxh_high)[None] + run_v, 0.0)
        edge = hy[3, vx] + jnp.where(inside_edge, cost(c0, c1, c2, vxh, vy_hat_edge), 0.0)
        lower, upper = both_vy(here, edge)
        grad_x = 0.5 * (above - below)
        grad_y = 0.5 * (upper - lower)
        laplace = above + below + upper + lower - 4.0 * here
        speed_x = jnp.abs(advect_rate * vxh)
        moved = wz[vx] + speed_x * cost(x0[None], x1[None], x2[None], vxh, vy_hat)
        moved = moved + speed_y * cost(y0[None], y1[None], y2[None], vxh, vy_hat)
        moved = moved - (speed_x + speed_y) * here
        new = here + moved - hamilton_rate * (grad_x * grad_x + grad_y * grad_y) + diffusion * laplace
        vo_ref[vx] = new + cost(e0[None], e1[None], e2[None], vxh, vy_hat)
        return 0

    lax.fori_loop(0, BX, last_step, 0)

    for c in sent:
        c.wait_send()
    for make in (make_u, make_1, make_z, make_2):
        for q in range(PACK):
            make(q).wait_send()


def per_device(density_start, value_guess, value_end, walls):
    field_shape = (BX, TILES, 8, 128)

    def tiled(a):
        return a.reshape(field_shape)

    vmem = pl.BlockSpec(memory_space=pltpu.VMEM)

    def slabs(n):
        return pltpu.VMEM((n, TILES, 8, 128), F32)

    def stacks(n, m):
        return pltpu.VMEM((n, m, TILES, 8, 128), F32)

    out = jax.ShapeDtypeStruct(field_shape, F32)
    density_end, value_start = pl.pallas_call(
        kernel,
        out_shape=(out, out),
        in_specs=[vmem] * 4,
        out_specs=(vmem, vmem),
        scratch_shapes=[
            slabs(18), slabs(18), slabs(20), slabs(18), slabs(16),
            pltpu.VMEM((16, 8, 128), F32),
            slabs(18), slabs(18), slabs(16), slabs(18), slabs(18), slabs(16), slabs(16),
            pltpu.VMEM((4, 16, 8, 128), F32),
            stacks(4, 4),
            pltpu.VMEM((4, 8, 8, 128), F32), pltpu.VMEM((4, 8, 8, 128), F32),
            pltpu.VMEM((8, 8, 8, 128), F32),
            stacks(4, 4),
            pltpu.VMEM((4, 16, 8, 128), F32),
            stacks(4, 4), stacks(4, 4),
            pltpu.VMEM((60, 2, 8, 128), F32),
            pltpu.VMEM((6, 8, 128), F32),
            pltpu.VMEM((2, 8, 128), jnp.int32),
            pltpu.SemaphoreType.DMA((112,)),
            pltpu.SemaphoreType.DMA((112,)),
        ],
        compiler_params=pltpu.CompilerParams(
            collective_id=0, has_side_effects=True, vmem_limit_bytes=40 * 1024 * 1024
        ),
    )(tiled(density_start), tiled(value_guess), tiled(value_end), walls)
    return density_end.reshape(density_start.shape), value_start.reshape(density_start.shape)


def solution(mesh):
    return jax.shard_map(
        per_device,
        mesh=mesh,
        in_specs=(
            P("vert", None, None, "gx", None),
            P("vert", None, None, "gx", None),
            P("vert", None, None, "gx", None),
            P("gx", None),
        ),
        out_specs=(P("vert", None, None, "gx", None), P("vert", None, None, "gx", None)),
        check_vma=False,
    )
```

time: 1230 us -> 110 us (0.09); the launches traced: 1220 us -> 110 us
  blocking collectives: 599 us -> 0 us
  starting transfers between devices: 317 us -> 0 us
  waiting for transfers between devices: 252 us -> 0 us
  Pallas kernels: 0 us -> 104 us
  other arithmetic: 19.6 us -> 0 us
  local copies, waits for them, and re-layouts: 24.3 us -> 5.39 us
    psum x3 -> x0, blocking collectives: 599 us -> none  [moment_stats(): total, mom_x, mom_y = lax.psum((total, mom_x, mom_y), 'vert')]
    ppermute x40 -> x0, starting transfers between devices: 317 us -> none  [the longest x12 116 us: partner_2(): return lax.ppermute(block, axis, route)]
    ppermute x40 -> x0, waiting for transfers between devices: 252 us -> none  [the longest x12 243 us: partner_2(): return lax.ppermute(block, axis, route)]
    pallas_call x0 -> x1, Pallas kernels: none -> 104 us  [per_device(): pl.pallas_call(kernel, out_shape=(out, out), in_specs=[vmem] * 4, out_spe...]
    slice x41 -> x0, local copies, waits for them, and re-layouts: 19.1 us -> none  [the longest x4 4.78 us: forward_step(): jnp.roll(field, -1, axis=4) - field]
  transfers between devices with their start and end apart: 40 -> 0, of which waited for: 13 -> 0; matrix products, arithmetic and copies ran while one was open for 2% -> 0% of each run, Pallas kernels for 0% -> 0%
where the time goes in v1:
time: 110 us
  Pallas kernels  104 us (95%)
  local copies, waits for them, and re-layouts  5.39 us (5%)
    pallas_call x1, Pallas kernels, per_device(): pl.pallas_call(kernel, out_shape=(out, out), in_specs=[vmem] * 4, out_spe...  104 us
    unnamed x10, local copies, waits for them, and re-layouts  5.39 us

profile of v1, /device:TPU:1, one launch (start us, length us, event | category | flops | bytes accessed | tf_op | source)
XLA Modules:
  0.0 109.7 jit_solution(13935549080331531277)
XLA Ops:
  0.6 0.0 copy-start.3
  0.6 0.7 copy-done.3
  1.3 0.0 copy-start
  1.3 1.0 copy-done
  2.4 0.0 copy-start.1
  2.4 1.0 copy-done.1
  3.4 0.0 copy-start.2
  3.4 1.0 copy-done.2
  4.4 103.7 %shard_map.59 = (f32[16,8,8,128]{3,2,1,0:T(8,128)S(1)}, f32[16,8,8,128]{3,2,1,0:T(8,128)S(1)}) custom-call(f32[16,8,8,128]{3,2,1,0:T(8,128)S(1)} %bitcast.5, f32[16,8,8,128]{3,2,1,0:T(8,128)S(1)} %bitcast.6, f32[16,8,8,128]{3,2,1,0:T(8,128)S(1)} %bitcast.7, s32[4,128]{1,0:T(4,128)S(1)} %copy-done.3), custom_call_target="tpu_custom_call" | custom-call | tf_op jit(solution)/shard_map/pallas_call | solution.py:570
  108.1 0.8 copy.8
  108.9 0.8 copy.9
Async XLA Ops:
  0.6 0.7 copy-start.3
  1.3 1.0 copy-start
  2.4 1.0 copy-start.1
  3.4 1.0 copy-start.2

commit v2 on v1

--- a/solution.py
+++ b/solution.py
@@ -17,6 +17,7 @@
 BX = 16
 BY = 16
 TILES = 8
+EARLY = 3
 PACK = 4
 
 advect_rate = 0.3
@@ -33,10 +34,10 @@
 
 
 def kernel(
-    m_ref, g_ref, u_ref, walls_ref, mo_ref, vo_ref,
-    mext, mext2, gext, gradx, grady, gradh, upx, dnx, field, uext, vext, pre, wz,
-    hy, xh, ylo, yhi, ysend, xsend, gvy, csend, crecv, red, tiles, idx,
-    send_sem, recv_sem,
+    m_hbm, g_hbm, u_hbm, walls_hbm, mo_ref, vo_ref,
+    mext, mext2, gext, gradx, grady, gradh, upx, dnx, upy, dny, base, field, uext, vext, pre, wz,
+    hy, xh, ylo, yhi, ysend, xsend, gvy, csend, crecv, red, idx, walls_ref,
+    send_sem, recv_sem, load_sem,
 ):
     vert = lax.axis_index("vert")
     gx = lax.axis_index("gx")
@@ -60,8 +61,17 @@
     x_up = {"gx": (gx + 1) % gx_count}
     x_down = {"gx": (gx + gx_count - 1) % gx_count}
 
+    loads = [
+        pltpu.make_async_copy(m_hbm, mext.at[pl.ds(1, BX)], load_sem.at[0]),
+        pltpu.make_async_copy(walls_hbm, walls_ref, load_sem.at[1]),
+        pltpu.make_async_copy(u_hbm, uext.at[pl.ds(1, BX)], load_sem.at[2]),
+        pltpu.make_async_copy(g_hbm, gext.at[pl.ds(2, BX)], load_sem.at[3]),
+    ]
+    for load in loads:
+        load.start()
+
     barrier = pltpu.get_barrier_semaphore()
-    roles = plane + depth + [mirror, vy_up, vy_down, x_up, x_down]
+    roles = depth + [mirror, vy_up, vy_down] + plane + [x_up, x_down]
     for peer in roles:
         pl.semaphore_signal(barrier, inc=1, device_id=peer, device_id_type=MESH)
 
@@ -92,13 +102,17 @@
         zero = jnp.zeros((8, 128), F32)
         return lax.fori_loop(0, BX, body, (zero, zero, zero))
 
-    def put_moments(slot, sums):
+    def put_moments(slot, sums, mom_y_cells=None):
         total, mom_x, mom_y = (a + roll4(a) for a in sums)
+        if mom_y_cells is not None:
+            mom_y = jnp.where(mom_y_cells, mom_y, 0.0)
         red[slot, 0] = jnp.where(lo8, total, mom_x)
         red[slot, 1] = mom_y
 
-    put_moments(0, local_moments(lambda vx: m_ref[vx]))
-
+    loads[0].wait()
+    put_moments(0, local_moments(lambda vx: mext[vx + 1]))
+
+    loads[1].wait()
     w4 = walls_ref[...]
     wall = jnp.concatenate([w4, w4], axis=0) == 1
     ones = wall.astype(F32)
@@ -121,7 +135,6 @@
     def along_y(slab, index):
         return jnp.take_along_axis(slab, jnp.broadcast_to(index[None], shape), axis=2)
 
-    pl.semaphore_wait(barrier, len(roles))
 
     counter = [0]
 
@@ -145,34 +158,37 @@
         for c in copies:
             c.wait_recv()
 
-    def plane_start(r):
+    def sums(r, slot):
+        return red.at[slot] if r == 2 else red.at[slot, pl.ds(0, 2)]
+
+    def depth_start(r, own=None):
         base = 20 * r
-        return [start(red.at[base], red.at[base + 1 + d], peer) for d, peer in enumerate(plane)]
+        own = base if own is None else own
+        return [start(sums(r, own), sums(r, base + 1 + d), peer) for d, peer in enumerate(depth)]
+
+    def plane_start(r, copies, own=None):
+        base = 20 * r
+        arrive(copies)
+        tiles = 3 if r == 2 else 2
+        acc = red[base if own is None else own, :tiles]
+        for d in range(3):
+            acc = acc + red[base + 1 + d, :tiles]
+        red[base + 4, :tiles] = acc
+        return [start(sums(r, base + 4), sums(r, base + 5 + d), peer) for d, peer in enumerate(plane)]
 
     def plane_finish(r, copies):
         base = 20 * r
         arrive(copies)
-        acc = red[base]
+        tiles = 3 if r == 2 else 2
+        acc = red[base + 4, :tiles]
         for d in range(15):
-            acc = acc + red[base + 1 + d]
-        red[base + 16] = acc
-        return [start(red.at[base + 16], red.at[base + 17 + d], peer) for d, peer in enumerate(depth)]
-
-    def depth_finish(r, copies, reflected):
-        base = 20 * r
-        arrive(copies)
-        acc = red[base + 16]
-        for d in range(3):
-            acc = acc + red[base + 17 + d]
+            acc = acc + red[base + 5 + d, :tiles]
         swapped = roll4(acc[0])
         total = jnp.where(lo8, acc[0], swapped)
         mom_x = jnp.where(lo8, swapped, acc[0])
-        mean_y = acc[1] / total
-        if reflected:
-            mean_y = jnp.where(wall, 0.0, mean_y)
-        return total, mom_x / total, mean_y
-
-    def vy_faces(slot, read):
+        return (total, mom_x / total, acc[1] / total), acc[tiles - 1]
+
+    def vy_pack(slot, read):
         def body(p, _):
             a0, a1 = read(2 * p, TILES - 1), read(2 * p + 1, TILES - 1)
             ysend[slot, p] = jnp.where(lo8, roll4(a0), a1)
@@ -181,6 +197,8 @@
             return 0
 
         lax.fori_loop(0, BX // 2, body, 0)
+
+    def vy_send(slot):
         return [
             start(ysend.at[slot], ylo.at[slot // 2], vy_up),
             start(ysend.at[slot + 1], yhi.at[slot // 2], vy_down),
@@ -208,7 +226,7 @@
         ext[0] = jnp.where(i == 0, 0.0, ext[0])
         ext[BX + 1] = jnp.where(i == KX - 1, 0.0, ext[BX + 1])
 
-    def x_faces(slot, read, below):
+    def x_pack(slot, read, below):
         def body(q, _):
             face = None
             for b in range(PACK):
@@ -241,6 +259,10 @@
         upper = jnp.where(lo8[None], r, jnp.concatenate([r[1:], edge[None]], axis=0))
         return lower, upper
 
+    def x_send(slot, below):
+        peer = {"gx": jnp.where(below, (gx + 1) % gx_count, (gx + gx_count - 1) % gx_count)}
+        return start(xsend.at[slot], xh.at[slot], peer)
+
     def mirror_copies(slot):
         n = counter[0]
         counter[0] += PACK
@@ -258,11 +280,10 @@
         taken = along_y(slab, idx[0])
         return taken if face is None else jnp.where((lane // 32 == b)[None], taken, face)
 
-    def send_packed(slot, q, face, make):
+    def turn(slot, q, face):
         turned = roll4(face)
         for t in range(TILES):
             csend[slot, q, t] = turned[TILES - 1 - t]
-        make(q).start()
 
     def reflect(slot, make, read, write):
         def body(q, carry):
@@ -277,90 +298,109 @@
 
         lax.fori_loop(0, PACK, body, 0)
 
-    def forward(ext, slot, xslot, stats, write, cslot):
+    def x_rates(ext, e, mean_x):
+        cells = ext[e]
+        drift = drift_limit * jnp.tanh((mean_x - vx_hat(e - 1))[None] - gradx[e])
+        upx[e] = cells * (diffusion + jnp.maximum(drift, 0.0))
+        dnx[e] = cells * (diffusion + jnp.maximum(-drift, 0.0))
+
+    def outflow(ext, stats):
         total, mean_x, mean_y = stats
 
-        def rates(e, _):
-            cells = ext[e]
-            drift = drift_limit * jnp.tanh((mean_x - vx_hat(e - 1))[None] - gradx[e])
-            upx[e] = cells * (diffusion + jnp.maximum(drift, 0.0))
-            dnx[e] = cells * (diffusion + jnp.maximum(-drift, 0.0))
+        def body(vx, _):
+            x_rates(ext, vx + 1, mean_x)
+            cells = ext[vx + 1]
+            drift = drift_limit * jnp.tanh(mean_y[None] - vy_hat - grady[vx])
+            upy[vx] = cells * (diffusion + jnp.maximum(drift, 0.0))
+            dny[vx] = cells * (diffusion + jnp.maximum(-drift, 0.0))
             return 0
 
-        lax.fori_loop(0, BX + 2, rates, 0)
-        make = mirror_copies(cslot)
+        lax.fori_loop(0, BX, body, 0)
+
+    def stay(ext, xslot):
+        step_x, step_y = 2.0 / VX, 2.0 / VY
+        top_y = jnp.where(jnp.logical_and(j == KY - 1, row >= 4), 1.0, 0.0)
+        bottom_y = jnp.where(jnp.logical_and(j == 0, row < 4), 1.0, 0.0)
 
         def body(q, carry):
             total, mom_x, mom_y = carry
+            for b in range(PACK):
+                vx = PACK * q + b
+                cells = ext[vx + 1]
+                up_x, down_x, up_y, down_y = upx[vx + 1], dnx[vx + 1], upy[vx], dny[vx]
+                speed_x = jnp.abs(advect_rate * vx_hat(vx))
+                moved = speed_x * (cells - x_neighbour(cells, xslot, q, b, high_x))
+                moved = moved + speed_y * (cells - y_neighbour(cells, high_y))
+                kept = cells - moved
+                base[vx] = kept - (up_x + down_x + up_y + down_y)
+                s = jnp.sum(kept, axis=0)
+                lost_up, lost_down = top_y * up_y[TILES - 1], bottom_y * down_y[0]
+                total = total + s - (lost_up + lost_down)
+                mom_x = mom_x + vx_hat(vx) * (s - (lost_up + lost_down)) + step_x * jnp.sum(up_x - down_x, axis=0)
+                mom_y = mom_y + jnp.sum(vy_hat * kept + step_y * (up_y - down_y), axis=0)
+                mom_y = mom_y - vy_hat_edge * (lost_up + lost_down)
+            return total, mom_x, mom_y
+
+        zero = jnp.zeros((8, 128), F32)
+        total, mom_x, mom_y = lax.fori_loop(0, PACK, body, (zero, zero, zero))
+        lost_up = jnp.where(i == KX - 1, 1.0, 0.0) * upx[BX]
+        lost_down = jnp.where(i == 0, 1.0, 0.0) * dnx[1]
+        s_up, s_down = jnp.sum(lost_up, axis=0), jnp.sum(lost_down, axis=0)
+        total = total - (s_up + s_down)
+        mom_x = mom_x - vx_hat(jnp.int32(BX)) * s_up - vx_hat(jnp.int32(-1)) * s_down
+        mom_y = mom_y - jnp.sum(vy_hat * (lost_up + lost_down), axis=0)
+        return total, mom_x, mom_y
+
+    def inflow(ext, hslot, stats, write, cslot):
+        total, mean_x, mean_y = stats
+        x_rates(ext, 0, mean_x)
+        x_rates(ext, BX + 1, mean_x)
+
+        def body(q, _):
             face = None
             for b in range(PACK):
                 vx = PACK * q + b
-                cells = ext[vx + 1]
-                drift = drift_limit * jnp.tanh(mean_y[None] - vy_hat - grady[vx])
-                up = cells * (diffusion + jnp.maximum(drift, 0.0))
-                down = cells * (diffusion + jnp.maximum(-drift, 0.0))
-                drift_e = drift_limit * jnp.tanh(mean_y - vy_hat_edge - gradh[vx])
-                cells_e = hy[slot // 2, vx]
-                up_e = cells_e * (diffusion + jnp.maximum(drift_e, 0.0))
-                down_e = cells_e * (diffusion + jnp.maximum(-drift_e, 0.0))
-                lower, upper = vy_neighbours(up, down, up_e, down_e)
-                flow = upx[vx] + dnx[vx + 2] + lower + upper - (upx[vx + 1] + dnx[vx + 1] + up + down)
-                speed_x = jnp.abs(advect_rate * vx_hat(vx))
-                moved = speed_x * (cells - x_neighbour(cells, xslot, q, b, high_x))
-                moved = moved + speed_y * (cells - y_neighbour(cells, high_y))
-                new = cells + flow - moved
+                drift = drift_limit * jnp.tanh(mean_y - vy_hat_edge - gradh[vx])
+                cells = hy[hslot, vx]
+                up_edge = cells * (diffusion + jnp.maximum(drift, 0.0))
+                down_edge = cells * (diffusion + jnp.maximum(-drift, 0.0))
+                lower, upper = vy_neighbours(upy[vx], dny[vx], up_edge, down_edge)
+                new = base[vx] + upx[vx] + dnx[vx + 2] + lower + upper
                 write(vx, new)
-                s = jnp.sum(new, axis=0)
-                total = total + s
-                mom_x = mom_x + vx_hat(vx) * s
-                mom_y = mom_y + jnp.sum(vy_hat * new, axis=0)
                 face = packed(face, new, b)
-            send_packed(cslot, q, face, make)
-            return total, mom_x, mom_y
-
-        zero = jnp.zeros((8, 128), F32)
-        sums = lax.fori_loop(0, PACK, body, (zero, zero, zero))
-        return sums, make
-
-    plane0 = plane_start(0)
-
-    def fill(ext, ref, lead):
-        def body(vx, _):
-            ext[vx + lead] = ref[vx]
+            turn(cslot, q, face)
             return 0
 
-        lax.fori_loop(0, BX, body, 0)
-
-    fill(uext, u_ref, 1)
+        lax.fori_loop(0, PACK, body, 0)
+
+    vy_pack(2, lambda vx, t: mext[vx + 1, t])
+    x_pack(1, lambda vx: mext[vx + 1], high_x)
+    loads[2].wait()
+    vy_pack(0, lambda vx, t: uext[vx + 1, t])
+    x_pack(0, lambda vx: uext[vx + 1], jnp.logical_not(high_x))
+    loads[3].wait()
+
+    def fill_g(vx, _):
+        gvy[0, vx] = gext[vx + 2, TILES - 1]
+        gvy[1, vx] = gext[vx + 2, 0]
+        return 0
+
+    lax.fori_loop(0, BX, fill_g, 0)
+    pl.semaphore_wait(barrier, len(roles))
+
+    depth0 = depth_start(0)
+    u_vy = vy_send(0)
     u_vx = vx_faces(uext)
-    u_vy = vy_faces(0, lambda vx, t: u_ref[vx, t])
-    x_faces(0, lambda vx: u_ref[vx], jnp.logical_not(high_x))
-
-    def x_send(slot, below):
-        peer = {"gx": jnp.where(below, (gx + 1) % gx_count, (gx + gx_count - 1) % gx_count)}
-        return start(xsend.at[slot], xh.at[slot], peer)
-
     u_x = x_send(0, jnp.logical_not(high_x))
-    fill(gext, g_ref, 2)
+    m_vy = vy_send(2)
+    g_vy = [start(gvy.at[0], gvy.at[2], vy_up), start(gvy.at[1], gvy.at[3], vy_down)]
+    m_vx = vx_faces(mext)
     g_vx = [
         start(gext.at[pl.ds(BX, 2)], gext.at[pl.ds(0, 2)], vx_up),
         start(gext.at[pl.ds(2, 2)], gext.at[pl.ds(BX + 2, 2)], vx_down),
     ]
-    fill(mext, m_ref, 1)
-    m_vx = vx_faces(mext)
-    m_vy = vy_faces(2, lambda vx, t: m_ref[vx, t])
-    x_faces(1, lambda vx: m_ref[vx], high_x)
     m_x = x_send(1, high_x)
-
-    def fill_g(vx, _):
-        gvy[0, vx] = g_ref[vx, TILES - 1]
-        gvy[1, vx] = g_ref[vx, 0]
-        return 0
-
-    lax.fori_loop(0, BX, fill_g, 0)
-    g_vy = [start(gvy.at[0], gvy.at[2], vy_up), start(gvy.at[1], gvy.at[3], vy_down)]
-
-    depth0 = plane_finish(0, plane0)
+    plane0 = plane_start(0, depth0)
 
     vx_halo(uext, u_vx)
     vy_halo(0, u_vy)
@@ -382,7 +422,8 @@
             new = here + moved - hamilton_rate * (grad_x * grad_x + grad_y * grad_y) + diffusion * laplace
             pre[vx] = new
             face = packed(face, new, b)
-        send_packed(0, q, face, make_u)
+        turn(0, q, face)
+        make_u(q).start()
         return 0
 
     lax.fori_loop(0, PACK, value_step, 0)
@@ -414,32 +455,31 @@
     vx_halo(mext, m_vx)
     vy_halo(2, m_vy)
     arrive([m_x])
-    stats0 = depth_finish(0, depth0, False)
+    stats0, _ = plane_finish(0, plane0)
+    outflow(mext, stats0)
+    put_moments(20, stay(mext, 1), jnp.logical_not(wall))
+    depth1 = depth_start(1)
 
     def write_field(vx, slab):
         field[vx] = slab
 
-    sums1, make_1 = forward(mext, 2, 1, stats0, write_field, 1)
-    put_moments(20, sums1)
-    plane1 = plane_start(1)
+    inflow(mext, 1, stats0, write_field, 1)
+    make_1 = mirror_copies(1)
+    for q in range(EARLY):
+        make_1(q).start()
 
     def write_v(vx, slab):
         vext[vx + 1] = slab
 
+    plane1 = plane_start(1, depth1)
+    for q in range(EARLY, PACK):
+        make_1(q).start()
     reflect(0, make_u, lambda vx: pre[vx], write_v)
+    x_pack(2, lambda vx: vext[vx + 1], jnp.logical_not(high_x))
+    v_x = x_send(2, jnp.logical_not(high_x))
     v_vx = vx_faces(vext)
-    x_faces(2, lambda vx: vext[vx + 1], jnp.logical_not(high_x))
-    v_x = x_send(2, jnp.logical_not(high_x))
-    depth1 = plane_finish(1, plane1)
-
-    def write_m(vx, slab):
-        mext2[vx + 1] = slab
-
-    reflect(1, make_1, lambda vx: field[vx], write_m)
-    n_vx = vx_faces(mext2)
-    n_vy = vy_faces(4, lambda vx, t: mext2[vx + 1, t])
-    x_faces(3, lambda vx: mext2[vx + 1], high_x)
-    n_x = x_send(3, high_x)
+    vy_pack(6, lambda vx, t: vext[vx + 1, t])
+    v_vy = vy_send(6)
 
     arrive([v_x])
     make_z = mirror_copies(2)
@@ -454,32 +494,57 @@
             moved = moved + speed_y * y_neighbour(here, jnp.logical_not(high_y))
             pre[vx] = moved
             face = packed(face, moved, b)
-        send_packed(2, q, face, make_z)
+        turn(2, q, face)
         return 0
 
     lax.fori_loop(0, PACK, transport_step, 0)
-    v_vy = vy_faces(6, lambda vx, t: vext[vx + 1, t])
-
-    stats1 = depth_finish(1, depth1, True)
+    for q in range(PACK):
+        make_z(q).start()
+
+    def write_m(vx, slab):
+        mext2[vx + 1] = slab
+
+    reflect(1, make_1, lambda vx: field[vx], write_m)
+    vy_pack(4, lambda vx, t: mext2[vx + 1, t])
+    n_vy = vy_send(4)
+    n_vx = vx_faces(mext2)
+    x_pack(3, lambda vx: mext2[vx + 1], high_x)
+    n_x = x_send(3, high_x)
+
+    stats1, _ = plane_finish(1, plane1)
+    outflow(mext2, stats1)
+    arrive([n_x])
+    put_moments(40, stay(mext2, 3), jnp.logical_not(wall))
+    arrive([start(sums(0, 40), sums(0, 60), x_up), start(sums(0, 40), sums(0, 61), x_down)])
+    third = jnp.zeros((8, 128), F32)
+    for k, (t, r) in enumerate(((0, 0), (0, 4), (1, 0))):
+        third = jnp.where(row == k, red[60, t, r + 3 : r + 4], third)
+        third = jnp.where(row == 3 + k, red[61, t, r : r + 1], third)
+    red[62, 0] = red[40, 0]
+    red[62, 1] = red[40, 1]
+    red[62, 2] = third
+    depth2 = depth_start(2, 62)
     vx_halo(mext2, n_vx)
     vy_halo(4, n_vy)
-    arrive([n_x])
 
     def write_out(vx, slab):
         mo_ref[vx] = slab
 
-    sums2, make_2 = forward(mext2, 4, 3, stats1, write_out, 3)
-    put_moments(40, sums2)
-    plane2 = plane_start(2)
+    inflow(mext2, 2, stats1, write_out, 3)
+    make_2 = mirror_copies(3)
+    for q in range(EARLY):
+        make_2(q).start()
 
     def write_z(vx, slab):
         wz[vx] = slab
 
     vx_halo(vext, v_vx)
     vy_halo(6, v_vy)
-    depth2 = plane_finish(2, plane2)
+    plane2 = plane_start(2, depth2, 62)
+    for q in range(EARLY, PACK):
+        make_2(q).start()
     reflect(2, make_z, lambda vx: pre[vx], write_z)
-    total2, mean_x2, mean_y2 = depth_finish(2, depth2, True)
+    (total2, mean_x2, mean_y2), near = plane_finish(2, plane2)
 
     half = 0.5 * time_step * velocity_cost
 
@@ -489,31 +554,23 @@
 
     c0, c1, c2 = coefficients(total2, mean_x2, mean_y2)
     e0, e1, e2 = coefficients(*stats1)
-    tiles[0] = c0
-    tiles[1] = c1
-    tiles[2] = c2
     back = jnp.logical_not(high_x)
-    stats_peer = {"gx": jnp.where(back, (gx + 1) % gx_count, (gx + gx_count - 1) % gx_count)}
-    stats_copy = start(tiles.at[pl.ds(0, 3)], tiles.at[pl.ds(3, 3)], stats_peer)
-
-    def write_end(vx, slab):
-        mo_ref[vx] = slab
-
-    reflect(3, make_2, lambda vx: mo_ref[vx], write_end)
-    arrive([stats_copy])
-
-    def x_tile(t):
-        here = tiles[t]
+    edge_row = row % 4 == jnp.where(back, 0, 3)
+
+    near_sums = [jnp.where(back, near[k : k + 1], near[3 + k : 4 + k]) for k in range(3)]
+    near_coefficients = coefficients(near_sums[0], near_sums[1] / near_sums[0], near_sums[2] / near_sums[0])
+
+    def x_tile(here, far):
         shifted = jnp.where(back, pltpu.roll(here, 1, axis=0), pltpu.roll(here, 7, axis=0))
-        far = jnp.where(back, pltpu.roll(tiles[3 + t], 5, axis=0), pltpu.roll(tiles[3 + t], 3, axis=0))
-        return jnp.where(row % 4 == jnp.where(back, 0, 3), far, shifted)
+        return jnp.where(edge_row, far, shifted)
 
     down_y = jnp.logical_not(high_y)
     near = jnp.where(down_y, 1, 127)
     away = jnp.where(down_y, 127, 1)
     y_near = [pltpu.roll(c, near, axis=1) for c in (c0, c1, c2)]
     y_away = [pltpu.roll(c, away, axis=1) for c in (c0, c1, c2)]
-    x0, x1, x2 = x_tile(0), x_tile(1), jnp.where(wall, 0.0, x_tile(2))
+    x0, x1, x2 = (x_tile(here, far) for here, far in zip((c0, c1, c2), near_coefficients))
+    x2 = jnp.where(wall, 0.0, x2)
     y0 = jnp.where(wall, 0.5 * (y_near[0] + y_away[0]), y_near[0])
     y1 = jnp.where(wall, 0.5 * (y_near[1] + y_away[1]), y_near[1])
     y2 = jnp.where(wall, 0.5 * (y_near[2] - y_away[2]), y_near[2])
@@ -545,6 +602,11 @@
 
     lax.fori_loop(0, BX, last_step, 0)
 
+    def write_end(vx, slab):
+        mo_ref[vx] = slab
+
+    reflect(3, make_2, lambda vx: mo_ref[vx], write_end)
+
     for c in sent:
         c.wait_send()
     for make in (make_u, make_1, make_z, make_2):
@@ -570,12 +632,13 @@
     density_end, value_start = pl.pallas_call(
         kernel,
         out_shape=(out, out),
-        in_specs=[vmem] * 4,
+        in_specs=[pl.BlockSpec(memory_space=pltpu.HBM)] * 4,
         out_specs=(vmem, vmem),
         scratch_shapes=[
             slabs(18), slabs(18), slabs(20), slabs(18), slabs(16),
             pltpu.VMEM((16, 8, 128), F32),
-            slabs(18), slabs(18), slabs(16), slabs(18), slabs(18), slabs(16), slabs(16),
+            slabs(18), slabs(18), slabs(16), slabs(16), slabs(16),
+            slabs(16), slabs(18), slabs(18), slabs(16), slabs(16),
             pltpu.VMEM((4, 16, 8, 128), F32),
             stacks(4, 4),
             pltpu.VMEM((4, 8, 8, 128), F32), pltpu.VMEM((4, 8, 8, 128), F32),
@@ -583,14 +646,15 @@
             stacks(4, 4),
             pltpu.VMEM((4, 16, 8, 128), F32),
             stacks(4, 4), stacks(4, 4),
-            pltpu.VMEM((60, 2, 8, 128), F32),
-            pltpu.VMEM((6, 8, 128), F32),
+            pltpu.VMEM((63, 3, 8, 128), F32),
             pltpu.VMEM((2, 8, 128), jnp.int32),
+            pltpu.VMEM((4, 128), jnp.int32),
             pltpu.SemaphoreType.DMA((112,)),
             pltpu.SemaphoreType.DMA((112,)),
+            pltpu.SemaphoreType.DMA((4,)),
         ],
         compiler_params=pltpu.CompilerParams(
-            collective_id=0, has_side_effects=True, vmem_limit_bytes=40 * 1024 * 1024
+            collective_id=0, has_side_effects=True, vmem_limit_bytes=60 * 1024 * 1024
         ),
     )(tiled(density_start), tiled(value_guess), tiled(value_end), walls)
     return density_end.reshape(density_start.shape), value_start.reshape(density_start.shape)

time: 110 us -> 102 us (0.927)
  Pallas kernels: 104 us -> 97.7 us
  local copies, waits for them, and re-layouts: 5.39 us -> 2.74 us
    pallas_call x1, Pallas kernels: 104 us -> 97.7 us  [per_device(): pl.pallas_call(kernel, out_shape=(out, out), in_specs=[pl.BlockSpec(memor...]
    unnamed x10 -> x4, local copies, waits for them, and re-layouts: 5.39 us -> 2.74 us
where the time goes in v2:
time: 102 us; the launch traced here: 101 us
  Pallas kernels  97.7 us (96%)
  local copies, waits for them, and re-layouts  2.74 us (3%)
    pallas_call x1, Pallas kernels, per_device(): pl.pallas_call(kernel, out_shape=(out, out), in_specs=[pl.BlockSpec(memor...  97.7 us
    unnamed x4, local copies, waits for them, and re-layouts  2.74 us

profile of v2, /device:TPU:1, one launch (start us, length us, event | category | flops | bytes accessed | tf_op | source)
XLA Modules:
  0.0 101.1 jit_solution(8199839954447652354)
XLA Ops:
  0.6 97.7 %shard_map.59 = (f32[16,8,8,128]{3,2,1,0:T(8,128)}, f32[16,8,8,128]{3,2,1,0:T(8,128)}) custom-call(f32[16,8,8,128]{3,2,1,0:T(8,128)} %bitcast.5, f32[16,8,8,128]{3,2,1,0:T(8,128)} %bitcast.6, f32[16,8,8,128]{3,2,1,0:T(8,128)} %bitcast.7, s32[4,128]{1,0:T(4,128)} %walls_hbm.1), custom_call_target="tpu_custom_call" | custom-call | tf_op jit(solution)/shard_map/pallas_call | solution.py:632
  98.3 0.0 copy-start
  98.4 1.9 %copy.8 = f32[1,16,16,4,128]{4,3,2,1,0:T(4,128)} copy(f32[1,16,16,4,128]{4,3,2,1,0:T(4,128)} %bitcast.9) | data formatting | bytes 1048576
  100.3 0.0 copy-done
  100.3 0.8 copy.9
Async XLA Ops:
  98.3 2.0 %copy-start = (f32[16,8,8,128]{3,2,1,0:T(8,128)S(1)}, f32[16,8,8,128]{3,2,1,0:T(8,128)}, u32[]{:S(2)}) copy-start(f32[16,8,8,128]{3,2,1,0:T(8,128)} %get-tuple-element.5) | copy-start | bytes 1572868

commit v3 on v2

--- a/solution.py
+++ b/solution.py
@@ -17,7 +17,7 @@
 BX = 16
 BY = 16
 TILES = 8
-EARLY = 3
+EARLY = (3, 1)
 PACK = 4
 
 advect_rate = 0.3
@@ -36,7 +36,7 @@
 def kernel(
     m_hbm, g_hbm, u_hbm, walls_hbm, mo_ref, vo_ref,
     mext, mext2, gext, gradx, grady, gradh, upx, dnx, upy, dny, base, field, uext, vext, pre, wz,
-    hy, xh, ylo, yhi, ysend, xsend, gvy, csend, crecv, red, idx, walls_ref,
+    hy, xh, ylo, yhi, ysend, xsend, gvy, csend, crecv, red, tiles, idx, walls_ref,
     send_sem, recv_sem, load_sem,
 ):
     vert = lax.axis_index("vert")
@@ -158,35 +158,29 @@
         for c in copies:
             c.wait_recv()
 
-    def sums(r, slot):
-        return red.at[slot] if r == 2 else red.at[slot, pl.ds(0, 2)]
-
-    def depth_start(r, own=None):
+    def depth_start(r):
         base = 20 * r
-        own = base if own is None else own
-        return [start(sums(r, own), sums(r, base + 1 + d), peer) for d, peer in enumerate(depth)]
-
-    def plane_start(r, copies, own=None):
+        return [start(red.at[base], red.at[base + 1 + d], peer) for d, peer in enumerate(depth)]
+
+    def plane_start(r, copies):
         base = 20 * r
         arrive(copies)
-        tiles = 3 if r == 2 else 2
-        acc = red[base if own is None else own, :tiles]
+        acc = red[base]
         for d in range(3):
-            acc = acc + red[base + 1 + d, :tiles]
-        red[base + 4, :tiles] = acc
-        return [start(sums(r, base + 4), sums(r, base + 5 + d), peer) for d, peer in enumerate(plane)]
+            acc = acc + red[base + 1 + d]
+        red[base + 4] = acc
+        return [start(red.at[base + 4], red.at[base + 5 + d], peer) for d, peer in enumerate(plane)]
 
     def plane_finish(r, copies):
         base = 20 * r
         arrive(copies)
-        tiles = 3 if r == 2 else 2
-        acc = red[base + 4, :tiles]
+        acc = red[base + 4]
         for d in range(15):
-            acc = acc + red[base + 5 + d, :tiles]
+            acc = acc + red[base + 5 + d]
         swapped = roll4(acc[0])
         total = jnp.where(lo8, acc[0], swapped)
         mom_x = jnp.where(lo8, swapped, acc[0])
-        return (total, mom_x / total, acc[1] / total), acc[tiles - 1]
+        return total, mom_x / total, acc[1] / total
 
     def vy_pack(slot, read):
         def body(p, _):
@@ -455,7 +449,7 @@
     vx_halo(mext, m_vx)
     vy_halo(2, m_vy)
     arrive([m_x])
-    stats0, _ = plane_finish(0, plane0)
+    stats0 = plane_finish(0, plane0)
     outflow(mext, stats0)
     put_moments(20, stay(mext, 1), jnp.logical_not(wall))
     depth1 = depth_start(1)
@@ -465,14 +459,14 @@
 
     inflow(mext, 1, stats0, write_field, 1)
     make_1 = mirror_copies(1)
-    for q in range(EARLY):
+    for q in range(EARLY[0]):
         make_1(q).start()
 
     def write_v(vx, slab):
         vext[vx + 1] = slab
 
     plane1 = plane_start(1, depth1)
-    for q in range(EARLY, PACK):
+    for q in range(EARLY[0], PACK):
         make_1(q).start()
     reflect(0, make_u, lambda vx: pre[vx], write_v)
     x_pack(2, lambda vx: vext[vx + 1], jnp.logical_not(high_x))
@@ -511,19 +505,11 @@
     x_pack(3, lambda vx: mext2[vx + 1], high_x)
     n_x = x_send(3, high_x)
 
-    stats1, _ = plane_finish(1, plane1)
+    stats1 = plane_finish(1, plane1)
     outflow(mext2, stats1)
     arrive([n_x])
     put_moments(40, stay(mext2, 3), jnp.logical_not(wall))
-    arrive([start(sums(0, 40), sums(0, 60), x_up), start(sums(0, 40), sums(0, 61), x_down)])
-    third = jnp.zeros((8, 128), F32)
-    for k, (t, r) in enumerate(((0, 0), (0, 4), (1, 0))):
-        third = jnp.where(row == k, red[60, t, r + 3 : r + 4], third)
-        third = jnp.where(row == 3 + k, red[61, t, r : r + 1], third)
-    red[62, 0] = red[40, 0]
-    red[62, 1] = red[40, 1]
-    red[62, 2] = third
-    depth2 = depth_start(2, 62)
+    depth2 = depth_start(2)
     vx_halo(mext2, n_vx)
     vy_halo(4, n_vy)
 
@@ -532,7 +518,7 @@
 
     inflow(mext2, 2, stats1, write_out, 3)
     make_2 = mirror_copies(3)
-    for q in range(EARLY):
+    for q in range(EARLY[1]):
         make_2(q).start()
 
     def write_z(vx, slab):
@@ -540,11 +526,11 @@
 
     vx_halo(vext, v_vx)
     vy_halo(6, v_vy)
-    plane2 = plane_start(2, depth2, 62)
-    for q in range(EARLY, PACK):
+    plane2 = plane_start(2, depth2)
+    for q in range(EARLY[1], PACK):
         make_2(q).start()
     reflect(2, make_z, lambda vx: pre[vx], write_z)
-    (total2, mean_x2, mean_y2), near = plane_finish(2, plane2)
+    total2, mean_x2, mean_y2 = plane_finish(2, plane2)
 
     half = 0.5 * time_step * velocity_cost
 
@@ -554,23 +540,24 @@
 
     c0, c1, c2 = coefficients(total2, mean_x2, mean_y2)
     e0, e1, e2 = coefficients(*stats1)
+    for k, c in enumerate((c0, c1, c2)):
+        tiles[k] = c
     back = jnp.logical_not(high_x)
+    stats_copy = start(tiles.at[pl.ds(0, 3)], tiles.at[pl.ds(3, 3)], {"gx": jnp.where(back, (gx + 1) % gx_count, (gx + gx_count - 1) % gx_count)})
     edge_row = row % 4 == jnp.where(back, 0, 3)
 
-    near_sums = [jnp.where(back, near[k : k + 1], near[3 + k : 4 + k]) for k in range(3)]
-    near_coefficients = coefficients(near_sums[0], near_sums[1] / near_sums[0], near_sums[2] / near_sums[0])
-
-    def x_tile(here, far):
-        shifted = jnp.where(back, pltpu.roll(here, 1, axis=0), pltpu.roll(here, 7, axis=0))
-        return jnp.where(edge_row, far, shifted)
+    def x_tile(here):
+        return jnp.where(back, pltpu.roll(here, 1, axis=0), pltpu.roll(here, 7, axis=0))
+
+    def x_far(t):
+        return jnp.where(back, pltpu.roll(tiles[3 + t], 5, axis=0), pltpu.roll(tiles[3 + t], 3, axis=0))
 
     down_y = jnp.logical_not(high_y)
     near = jnp.where(down_y, 1, 127)
     away = jnp.where(down_y, 127, 1)
     y_near = [pltpu.roll(c, near, axis=1) for c in (c0, c1, c2)]
     y_away = [pltpu.roll(c, away, axis=1) for c in (c0, c1, c2)]
-    x0, x1, x2 = (x_tile(here, far) for here, far in zip((c0, c1, c2), near_coefficients))
-    x2 = jnp.where(wall, 0.0, x2)
+    x0, x1, x2 = x_tile(c0), x_tile(c1), jnp.where(wall, 0.0, x_tile(c2))
     y0 = jnp.where(wall, 0.5 * (y_near[0] + y_away[0]), y_near[0])
     y1 = jnp.where(wall, 0.5 * (y_near[1] + y_away[1]), y_near[1])
     y2 = jnp.where(wall, 0.5 * (y_near[2] - y_away[2]), y_near[2])
@@ -593,7 +580,8 @@
         grad_y = 0.5 * (upper - lower)
         laplace = above + below + upper + lower - 4.0 * here
         speed_x = jnp.abs(advect_rate * vxh)
-        moved = wz[vx] + speed_x * cost(x0[None], x1[None], x2[None], vxh, vy_hat)
+        inner = speed_x * cost(x0[None], x1[None], x2[None], vxh, vy_hat)
+        moved = wz[vx] + jnp.where(edge_row[None], 0.0, inner)
         moved = moved + speed_y * cost(y0[None], y1[None], y2[None], vxh, vy_hat)
         moved = moved - (speed_x + speed_y) * here
         new = here + moved - hamilton_rate * (grad_x * grad_x + grad_y * grad_y) + diffusion * laplace
@@ -602,10 +590,23 @@
 
     lax.fori_loop(0, BX, last_step, 0)
 
+    def edge_part():
+        arrive([stats_copy])
+        f0, f1, f2 = x_far(0), x_far(1), jnp.where(wall, 0.0, x_far(2))
+
+        def edge_step(vx, _):
+            vxh = vx_hat(vx)
+            outer = jnp.abs(advect_rate * vxh) * cost(f0[None], f1[None], f2[None], vxh, vy_hat)
+            vo_ref[vx] = vo_ref[vx] + jnp.where(edge_row[None], outer, 0.0)
+            return 0
+
+        lax.fori_loop(0, BX, edge_step, 0)
+
     def write_end(vx, slab):
         mo_ref[vx] = slab
 
     reflect(3, make_2, lambda vx: mo_ref[vx], write_end)
+    edge_part()
 
     for c in sent:
         c.wait_send()
@@ -646,7 +647,8 @@
             stacks(4, 4),
             pltpu.VMEM((4, 16, 8, 128), F32),
             stacks(4, 4), stacks(4, 4),
-            pltpu.VMEM((63, 3, 8, 128), F32),
+            pltpu.VMEM((60, 2, 8, 128), F32),
+            pltpu.VMEM((6, 8, 128), F32),
             pltpu.VMEM((2, 8, 128), jnp.int32),
             pltpu.VMEM((4, 128), jnp.int32),
             pltpu.SemaphoreType.DMA((112,)),

time: 102 us -> 100 us (0.980)
  Pallas kernels: 97.7 us -> 95.6 us
    pallas_call x1, Pallas kernels: 97.7 us -> 95.6 us  [per_device(): pl.pallas_call(kernel, out_shape=(out, out), in_specs=[pl.BlockSpec(memor...]
where the time goes in v3:
time: 100 us; the launch traced here: 99 us
  Pallas kernels  95.6 us (96%)
  local copies, waits for them, and re-layouts  2.74 us (3%)
    pallas_call x1, Pallas kernels, per_device(): pl.pallas_call(kernel, out_shape=(out, out), in_specs=[pl.BlockSpec(memor...  95.6 us
    unnamed x4, local copies, waits for them, and re-layouts  2.74 us

profile of v3, /device:TPU:1, one launch (start us, length us, event | category | flops | bytes accessed | tf_op | source)
XLA Modules:
  0.0 99.0 jit_solution(5677140522359304044)
XLA Ops:
  0.6 95.6 %shard_map.59 = (f32[16,8,8,128]{3,2,1,0:T(8,128)}, f32[16,8,8,128]{3,2,1,0:T(8,128)}) custom-call(f32[16,8,8,128]{3,2,1,0:T(8,128)} %bitcast.5, f32[16,8,8,128]{3,2,1,0:T(8,128)} %bitcast.6, f32[16,8,8,128]{3,2,1,0:T(8,128)} %bitcast.7, s32[4,128]{1,0:T(4,128)} %walls_hbm.1), custom_call_target="tpu_custom_call" | custom-call | tf_op jit(solution)/shard_map/pallas_call | solution.py:633
  96.2 0.0 copy-start
  96.2 1.9 %copy.8 = f32[1,16,16,4,128]{4,3,2,1,0:T(4,128)} copy(f32[1,16,16,4,128]{4,3,2,1,0:T(4,128)} %bitcast.9) | data formatting | bytes 1048576
  98.2 0.0 copy-done
  98.2 0.8 copy.9
Async XLA Ops:
  96.2 2.0 %copy-start = (f32[16,8,8,128]{3,2,1,0:T(8,128)S(1)}, f32[16,8,8,128]{3,2,1,0:T(8,128)}, u32[]{:S(2)}) copy-start(f32[16,8,8,128]{3,2,1,0:T(8,128)} %get-tuple-element.5) | copy-start | bytes 1572868

commit v4 on v3

--- a/solution.py
+++ b/solution.py
@@ -656,7 +656,7 @@
             pltpu.SemaphoreType.DMA((4,)),
         ],
         compiler_params=pltpu.CompilerParams(
-            collective_id=0, has_side_effects=True, vmem_limit_bytes=60 * 1024 * 1024
+            collective_id=0, has_side_effects=True, vmem_limit_bytes=53 * 1024 * 1024
         ),
     )(tiled(density_start), tiled(value_guess), tiled(value_end), walls)
     return density_end.reshape(density_start.shape), value_start.reshape(density_start.shape)

time: 100 us -> 99.3 us (level)
    unnamed x4 -> x6, local copies, waits for them, and re-layouts: 2.74 us -> 2.69 us
where the time goes in v4:
time: 99.3 us; the launch traced here: 98.7 us
  Pallas kernels  95.4 us (96%)
  local copies, waits for them, and re-layouts  2.69 us (3%)
    pallas_call x1, Pallas kernels, per_device(): pl.pallas_call(kernel, out_shape=(out, out), in_specs=[pl.BlockSpec(memor...  95.4 us
    unnamed x6, local copies, waits for them, and re-layouts  2.69 us

profile of v4, /device:TPU:1, one launch (start us, length us, event | category | flops | bytes accessed | tf_op | source)
XLA Modules:
  0.0 98.7 jit_solution(2527319638618180128)
XLA Ops:
  0.6 0.0 copy-start
  0.6 0.7 copy-done
  1.3 95.4 %shard_map.59 = (f32[16,8,8,128]{3,2,1,0:T(8,128)S(1)}, f32[16,8,8,128]{3,2,1,0:T(8,128)}) custom-call(f32[16,8,8,128]{3,2,1,0:T(8,128)} %bitcast.6, f32[16,8,8,128]{3,2,1,0:T(8,128)} %bitcast.7, f32[16,8,8,128]{3,2,1,0:T(8,128)} %bitcast.8, s32[4,128]{1,0:T(4,128)S(1)} %copy-done), custom_call_target="tpu_custom_call" | custom-call | tf_op jit(solution)/shard_map/pallas_call | solution.py:633
  96.7 0.0 copy-start.1
  96.7 0.8 copy.8
  97.5 0.4 copy-done.1
  97.9 0.8 copy.9
Async XLA Ops:
  0.6 0.7 copy-start
  96.7 1.2 %copy-start.1 = (f32[16,8,8,128]{3,2,1,0:T(8,128)S(1)}, f32[16,8,8,128]{3,2,1,0:T(8,128)}, u32[]{:S(2)}) copy-start(f32[16,8,8,128]{3,2,1,0:T(8,128)} %get-tuple-element.5) | copy-start | bytes 1572868
